TPU v7x, 32 devices: a whole 2x2x4 slice. The times are simulated.
32 devices in a mesh: wide: 8 (over z, y), narrow: 4 (over x, core).
Axes of the slice: x: 2, y: 2, z: 4, core: 2. Of those that a mesh axis runs over, the one named last changes fastest.
Arguments:
- features: bfloat16 [2048, 512], P('wide', 'narrow'), may hold values from -6 to 6
- tile_blocks: bfloat16 [8, 4, 48, 128, 128], P('wide', 'narrow'), may hold values from -0.078125 to 0.078125
- tile_rows: int32 [8, 4, 48], P('wide', 'narrow'), may hold values from 0 to 1
- tile_cols: int32 [8, 4, 48], P('wide', 'narrow'), may hold values from 0 to 3, as said below
- tile_count: int32 [8, 4], P('wide', 'narrow'), may hold values from 12 to 48, as said below
- neighbor_weight: bfloat16 [512, 512], P('narrow'), may hold values from -0.25 to 0.25
- root_weight: bfloat16 [512, 512], P('narrow'), may hold values from -0.25 to 0.25
- output_weight: bfloat16 [512, 512], replicated, may hold values from -0.25 to 0.25
- cotangent: bfloat16 [2048, 512], P('wide'), may hold values from -0.3125 to 0.3125
Outputs:
- layer_output: bfloat16 [2048, 512], P('wide', 'narrow')
- neighbor_grad: float32 [512, 512], P('narrow')
- root_grad: float32 [512, 512], P('narrow')
- output_grad: float32 [512, 512], P(None, 'narrow')
Inputs may be any that keep to these rules, and one draw needn't show every extreme that they name: `tile_count`: slots at or past a device's count hold no tiles and are ignored; the largest count is 48 on some device in every draw, the smallest max(1, 12) on another. `tile_cols`: positions may repeat; repeated tiles add. Slot 0 of every device of row block b names the column tile that holds the nodes of row block b + 8 // 2 (counted round).
All inputs are finite; a program needn't handle non-finite values.
Results may differ from a plain program's by a relative error of at most 0.015.
Values may be sent and summed in bfloat16 or wider, within the bound.
A program may use at most 64 MiB of HBM per device.

v0:
```python
import math

import jax
import jax.numpy as jnp
from jax import lax
from jax.sharding import PartitionSpec as P


def tile_sum(block_tiles, row_ids, col_ids, live_count, column_tiles, tile_rows_count):
    capacity = block_tiles.shape[0]
    block_size = math.gcd(capacity, 24)
    tile_side = block_tiles.shape[-1]
    feature_width = column_tiles.shape[-1]
    row_range = jnp.arange(tile_rows_count, dtype=jnp.int32)
    slot_range = jnp.arange(block_size, dtype=jnp.int32)

    def one_turn(turn_index, running):
        first_slot = turn_index * block_size
        some_tiles = lax.dynamic_slice_in_dim(block_tiles, first_slot, block_size, 0)
        some_rows = lax.dynamic_slice_in_dim(row_ids, first_slot, block_size, 0)
        some_cols = lax.dynamic_slice_in_dim(col_ids, first_slot, block_size, 0)
        picked = column_tiles[some_cols]
        product = jnp.einsum("tij,tjh->tih", some_tiles, picked, preferred_element_type=jnp.float32)
        alive = (first_slot + slot_range < live_count).astype(jnp.float32)
        placing = alive[:, None] * (some_rows[:, None] == row_range[None, :]).astype(jnp.float32)
        return running + jnp.einsum("tr,tih->rih", placing, product)

    block_turns = (live_count + block_size - 1) // block_size
    start_value = jnp.zeros((tile_rows_count, tile_side, feature_width), jnp.float32)
    summed = lax.fori_loop(0, block_turns, one_turn, start_value)
    return summed.reshape(tile_rows_count * tile_side, feature_width)


def per_device(
    features,
    tile_blocks,
    tile_rows,
    tile_cols,
    tile_count,
    neighbor_weight,
    root_weight,
    output_weight,
    cotangent,
):
    node_rows = features.shape[0]
    slice_width = features.shape[1]
    wide_count = lax.axis_size("wide")
    narrow_count = lax.axis_size("narrow")
    tile_side = tile_blocks.shape[-1]
    tile_rows_count = node_rows // tile_side
    group_rows = node_rows // narrow_count
    all_tiles, all_rows, all_cols, all_counts = (
        lax.all_gather(tile_blocks, "narrow", axis=1, tiled=True),
        lax.all_gather(tile_rows, "narrow", axis=1, tiled=True),
        lax.all_gather(tile_cols, "narrow", axis=1, tiled=True),
        lax.all_gather(tile_count, "narrow", axis=1, tiled=True),
    )
    columns = lax.all_gather(features, "wide", axis=0, tiled=True)
    groups = columns.reshape(wide_count, narrow_count, group_rows, slice_width).transpose(
        1, 0, 2, 3
    )
    groups = groups.reshape(narrow_count, -1, tile_side, slice_width)
    running = jnp.zeros((node_rows, slice_width), jnp.float32)
    for source in range(narrow_count):
        running = running + tile_sum(
            all_tiles[0, source],
            all_rows[0, source],
            all_cols[0, source],
            all_counts[0, source],
            groups[source],
            tile_rows_count,
        )
    agg = running.astype(jnp.bfloat16)
    partial_pre = jnp.dot(agg, neighbor_weight, preferred_element_type=jnp.float32) + jnp.dot(
        features, root_weight, preferred_element_type=jnp.float32
    )
    pre = lax.psum(partial_pre, "narrow")
    hidden = jax.nn.silu(pre).astype(jnp.bfloat16)
    narrow_index = lax.axis_index("narrow")
    out_columns = lax.dynamic_slice_in_dim(
        output_weight, narrow_index * slice_width, slice_width, 1
    )
    layer_output = (
        features.astype(jnp.float32)
        + jnp.dot(hidden, out_columns, preferred_element_type=jnp.float32)
    ).astype(jnp.bfloat16)
    hidden_grad = jnp.dot(cotangent, output_weight.T, preferred_element_type=jnp.float32)
    sigmoid_pre = jax.nn.sigmoid(pre)
    pre_grad = (hidden_grad * sigmoid_pre * (1.0 + pre * (1.0 - sigmoid_pre))).astype(jnp.bfloat16)
    cot_columns = lax.dynamic_slice_in_dim(cotangent, narrow_index * slice_width, slice_width, 1)
    neighbor_part = jnp.dot(agg.T, pre_grad, preferred_element_type=jnp.float32)
    root_part = jnp.dot(features.T, pre_grad, preferred_element_type=jnp.float32)
    output_part = jnp.dot(hidden.T, cot_columns, preferred_element_type=jnp.float32)
    neighbor_grad, root_grad, output_grad = lax.psum(
        (neighbor_part, root_part, output_part), "wide"
    )
    return (layer_output, neighbor_grad, root_grad, output_grad)


def solution(mesh):
    return jax.shard_map(
        per_device,
        mesh=mesh,
        in_specs=(
            P("wide", "narrow"),
            P("wide", "narrow", None, None, None),
            P("wide", "narrow", None),
            P("wide", "narrow", None),
            P("wide", "narrow"),
            P("narrow", None),
            P("narrow", None),
            P(),
            P("wide", None),
        ),
        out_specs=(P("wide", "narrow"), P("narrow", None), P("narrow", None), P(None, "narrow")),
        check_vma=False,
    )
```

profile of v0, /device:TPU:0, one launch (start us, length us, event | category | flops | bytes accessed | tf_op | source)
XLA Modules:
  0.0 220.4 jit_solution(8340367925133181440)
XLA Ops:
  9.9 6.4 %all-reduce = s32[4]{0:T(128)S(1)} all-reduce(s32[4]{0:T(128)S(1)} %bitcast_dynamic-update-slice_fusion), channel_id=1, replica_groups=mesh['wide'=8,'narrow'=4] {'narrow'}, use_global_device_ids=true, to_apply=%add | all-reduce | flops 4 | bytes 32
  19.7 31.7 %all_gather.19 = bf16[2048,128]{1,0:T(8,128)(2,1)S(1)} all-gather(bf16[256,128]{1,0:T(8,128)(2,1)S(1)} %copy-done.1), channel_id=1, replica_groups=mesh['wide'=8,'narrow'=4] {'wide'}, dimensions={0}, use_global_device_ids=true | all-gather | bytes 589824 | tf_op jit(solution)/shard_map/all_gather | solution.py:58
  51.5 5.0 %all_gather.16 = s32[1,4,48]{2,0,1:T(1,128)S(1)} all-gather(s32[1,1,48]{2,0,1:T(1,128)S(1)} %bitcast.100), channel_id=1, replica_groups=mesh['wide'=8,'narrow'=4] {'narrow'}, dimensions={1}, use_global_device_ids=true | all-gather | bytes 960 | tf_op jit(solution)/shard_map/all_gather | solution.py:54
  56.5 5.0 %all_gather.18 = s32[1,4,48]{2,0,1:T(1,128)S(1)} all-gather(s32[1,1,48]{2,0,1:T(1,128)S(1)} %bitcast.101), channel_id=1, replica_groups=mesh['wide'=8,'narrow'=4] {'narrow'}, dimensions={1}, use_global_device_ids=true | all-gather | bytes 960 | tf_op jit(solution)/shard_map/all_gather | solution.py:55
  62.8 6.6 %slice_bitcast_fusion.3 = (bf16[48,128,128]{2,1,0:T(8,128)(2,1)}, bf16[48,128,128]{2,1,0:T(8,128)(2,1)S(1)}, bf16[48,128,128]{2,1,0:T(8,128)(2,1)}, bf16[48,128,128]{2,1,0:T(8,128)(2,1)}) fusion(bf16[1,4,48,128,128]{4,3,2,0,1:T(8,128)(2,1)} %all-gather.2.cloned.1.call-done), kind=kLoop, calls=%fused_computation.83 | loop fusion | bytes 12582912 | tf_op jit(solution)/shard_map/squeeze | solution.py:66
  69.4 9.2 %while.44 = (s32[]{:T(128)}, f32[2,128,128]{2,0,1:T(2,128)S(1)}, s32[]{:T(128)}, s32[48]{0:T(128)}, s32[]{:T(128)}, /*index=5*/bf16[48,128,128]{2,1,0:T(8,128)(2...) while((s32[]{:T(128)}, f32[2,128,128]{2,0,1:T(2,128)S(1)}, ...), condition=%wide.region_1.2_spmd.clone, body=%wide.region_0.1_spmd.clone.sunk | while | flops 102270200 | bytes 4986579 | solution.py:30
  70.9 1.5 fusion.133
  73.2 0.8 fusion.134
  75.5 1.5 fusion.133
  77.7 0.8 fusion.134
  78.6 9.2 %while.45 = (s32[]{:T(128)}, f32[2,128,128]{2,0,1:T(2,128)S(1)}, s32[]{:T(128)}, s32[48]{0:T(128)}, s32[]{:T(128)}, /*index=5*/bf16[48,128,128]{2,1,0:T(8,128)(2...) while((s32[]{:T(128)}, f32[2,128,128]{2,0,1:T(2,128)S(1)}, ...), condition=%wide.region_3.4_spmd.clone, body=%wide.region_2.3_spmd.clone.sunk | while | flops 102270200 | bytes 4986579 | solution.py:30
  80.1 1.5 fusion.139
  82.4 0.8 fusion.140
  84.8 1.5 fusion.139
  87.0 0.8 fusion.140
  87.9 4.5 %while.46 = (s32[]{:T(128)}, f32[2,128,128]{2,0,1:T(2,128)S(1)}, s32[]{:T(128)}, s32[48]{0:T(128)S(1)}, s32[]{:T(128)}, /*index=5*/bf16[48,128,128]{2,1,0:T(8,12...) while((s32[]{:T(128)}, f32[2,128,128]{2,0,1:T(2,128)S(1)}, ...), condition=%wide.region_5.6_spmd.clone, body=%wide.region_4.5_spmd.clone.sunk | while | flops 102270200 | bytes 4985783 | solution.py:30
  89.4 1.5 fusion.145
  91.6 0.8 fusion.146
  92.5 2.8 %while.47 = (s32[]{:T(128)}, f32[2,128,128]{2,0,1:T(2,128)S(1)}, s32[]{:T(128)}, s32[48]{0:T(128)S(1)}, s32[]{:T(128)}, /*index=5*/bf16[48,128,128]{2,1,0:T(8,12...) while((s32[]{:T(128)}, f32[2,128,128]{2,0,1:T(2,128)S(1)}, ...), condition=%wide.region_7.8_spmd.clone, body=%wide.region_6.7_spmd.clone.sunk | while | flops 102270200 | bytes 4985783 | solution.py:30
  94.4 0.8 fusion.152
  95.3 1.1 fusion.87
  96.5 2.0 convolution_add_fusion
  98.5 30.3 %all-reduce.5.cloned.1.call-done = f32[256,512]{1,0:T(8,128)} async-done(((f32[256,512]{1,0:T(8,128)}), f32[256,512]{1,0:T(8,128)}) %all-reduce.5.cloned.1.call-update) | async-done | bytes 524304 | tf_op jit(solution)/shard_map/psum | solution.py:77
  128.8 1.5 fusion.77
  130.3 0.9 fusion.88
  131.2 1.0 convolution_bitcast_fusion
  132.3 1.0 fusion.81
  133.3 0.9 fusion.78
  134.2 74.5 %all-reduce.7.cloned.1.call-done = (f32[128,512]{1,0:T(8,128)}, f32[128,512]{0,1:T(8,128)}, f32[512,128]{1,0:T(8,128)}) async-done(((f32[128,512]{1,0:T(8,128)}, f32[128,512]{0,1:T(8,128)}, f32[512,128]{1,0:T(8,128)}), (f32[128,512]{1,0:T(8,128)}, f32[128,512]{0,1:T(8,128)}, f32[512,128]{1,0:T(8,128)})) %all-reduce.7.cloned.1.call-update) | async-done | bytes 786448 | tf_op jit(solution)/shard_map/psum | solution.py:94
  208.7 1.8 copy.33
  210.5 1.7 copy.100
  212.2 1.7 copy.101
  (76 shorter events, 17.2 us)
Async XLA Ops:
  7.2 121.6 %copy-start = (bf16[512,512]{1,0:T(8,128)(2,1)S(1)}, bf16[512,512]{1,0:T(8,128)(2,1)}, u32[]{:S(2)}) copy-start(bf16[512,512]{1,0:T(8,128)(2,1)} %param.24) | copy-start | bytes 1572868
  7.2 1.5 copy-start.9
  7.2 12.5 %copy-start.1 = (bf16[256,128]{1,0:T(8,128)(2,1)S(1)}, bf16[256,128]{1,0:T(8,128)(2,1)}, u32[]{:S(2)}) copy-start(bf16[256,128]{1,0:T(8,128)(2,1)} %param.17) | copy-start | bytes 196612
  7.2 55.6 %all-gather.2.cloned.1.call-start = ((), (), s32[]{:S(2)}) async-start(), calls=%async_computation | async-start | bytes 7864320 | tf_op jit(solution)/shard_map/all_gather | solution.py:53
  7.3 44.2 %copy-start.5 = (s32[1,1,48]{2,1,0:T(1,128)S(1)}, s32[1,1,48]{2,1,0:T(1,128)}, u32[]{:S(2)}) copy-start(s32[1,1,48]{2,1,0:T(1,128)} %param.19) | copy-start | bytes 580
  7.3 49.2 %copy-start.6 = (s32[1,1,48]{2,1,0:T(1,128)S(1)}, s32[1,1,48]{2,1,0:T(1,128)}, u32[]{:S(2)}) copy-start(s32[1,1,48]{2,1,0:T(1,128)} %param.20) | copy-start | bytes 580
  7.9 120.8 %all-reduce.5.cloned.1.call-start = ((), (), s32[]{:S(2)}) async-start(), calls=%async_computation.1 | async-start | bytes 1048576 | tf_op jit(solution)/shard_map/psum | solution.py:77
  70.9 1.5 copy-start.8
  75.5 1.5 copy-start.8
  80.1 1.5 copy-start.7
  84.7 1.5 copy-start.7
  95.3 33.5 %copy-start.4 = (bf16[256,512]{1,0:T(8,128)(2,1)S(1)}, bf16[256,512]{1,0:T(8,128)(2,1)}, u32[]{:S(2)}) copy-start(bf16[256,512]{1,0:T(8,128)(2,1)} %param.25) | copy-start | bytes 786436
  98.5 110.3 %all-reduce.7.cloned.1.call-start = ((), (), s32[]{:S(2)}) async-start(), calls=%async_computation.2 | async-start | bytes 1572864 | tf_op jit(solution)/shard_map/psum | solution.py:94
  98.5 32.7 %copy-start.2 = (bf16[256,128]{1,0:T(8,128)(2,1)S(1)}, bf16[256,128]{1,0:T(8,128)(2,1)}, u32[]{:S(2)}) copy-start(bf16[256,128]{1,0:T(8,128)(2,1)} %param.17) | copy-start | bytes 196612
  128.8 3.4 %copy-start.3 = (f32[256,512]{1,0:T(8,128)S(1)}, f32[256,512]{1,0:T(8,128)}, u32[]{:S(2)}) copy-start(f32[256,512]{1,0:T(8,128)} %all-reduce.5.cloned.1.call-done) | copy-start | bytes 1572868
Sparse Core Ops, SparseCore 0:
  9.6 49.1 all-gather.1
  98.6 30.1 all-reduce.4
  133.5 75.2 all-reduce.6
where the time goes:
time: 223 us; the launch traced here: 220 us
  waiting for transfers between devices  106 us (48%)
  blocking collectives  48.1 us (22%)
  matrix products  21.2 us (10%)
  local copies, waits for them, and re-layouts  19.8 us (9%)
  between operations  17.4 us (8%)
  other arithmetic  7.97 us (4%)
    psum x1, waiting for transfers between devices, per_device(): lax.psum((neighbor_part, root_part, output_part), 'wide')  74.5 us
    all_gather x1, blocking collectives, per_device(): columns = lax.all_gather(features, 'wide', axis=0, tiled=True)  31.7 us
    psum x1, waiting for transfers between devices, per_device(): pre = lax.psum(partial_pre, 'narrow')  30.3 us
    dot_general x6, matrix products, one_turn(): jnp.einsum('tij,tjh->tih', some_tiles, picked, preferred_element_type=jnp...  7.85 us
    squeeze x1, local copies, waits for them, and re-layouts, per_device(): all_tiles[0, source]  6.61 us
    unnamed x22, local copies, waits for them, and re-layouts  6.43 us
    unnamed x1, blocking collectives  6.39 us
    all_gather x1, blocking collectives, per_device(): lax.all_gather(tile_rows, 'narrow', axis=1, tiled=True)  5.04 us
  transfers between devices with their start and end apart: 3, of which 2 were waited for; matrix products, arithmetic and copies ran while one was open for 2% of the time, Pallas kernels for 0%

commit v1 on v0

--- a/solution.py
+++ b/solution.py
@@ -1,8 +1,11 @@
+import functools
 import math
 
 import jax
 import jax.numpy as jnp
 from jax import lax
+from jax.experimental import pallas as pl
+from jax.experimental.pallas import tpu as pltpu
 from jax.sharding import PartitionSpec as P
 
 
@@ -31,7 +34,7 @@
     return summed.reshape(tile_rows_count * tile_side, feature_width)
 
 
-def per_device(
+def per_device_large(
     features,
     tile_blocks,
     tile_rows,
@@ -97,7 +100,314 @@
     return (layer_output, neighbor_grad, root_grad, output_grad)
 
 
+Y_SIZE = 2
+CORES = 2
+MESH = pl.DeviceIdType.MESH
+
+
+def fused_kernel(
+    wide, narrow,
+    x_hbm, t_hbm, rows_ref, cols_ref, count_ref, wn_hbm, wr_hbm, ow_hbm, cot_hbm,
+    grads_out, lo_out,
+    x_vm, tiles, ow, cot, fg, weights, dense, part, part_bf, agg_in, agg_r, agg_cols,
+    pg, hid, grad32, grad, from_y, to_z, from_z, gall, lo,
+    local_sem, send_sem, recv_sem,
+):
+    z_size = wide // Y_SIZE
+    me_b = lax.axis_index("wide")
+    me_n = lax.axis_index("narrow")
+    z, y = me_b // Y_SIZE, me_b % Y_SIZE
+    other_y = 1 - y
+    core_n = me_n // CORES * CORES + (1 - me_n % CORES)
+    x_n = (me_n + CORES) % narrow
+    xc_n = (core_n + CORES) % narrow
+    node_rows = x_hbm.shape[0]
+    width = x_hbm.shape[1]
+    hidden_width = ow_hbm.shape[0]
+    group = node_rows // narrow
+    side = t_hbm.shape[-1]
+    slots = t_hbm.shape[2]
+    piece = gall.shape[1]
+    f32, bf16 = jnp.float32, jnp.bfloat16
+    y_dev = (z * Y_SIZE + other_y, me_n)
+
+    def group_rows(n):
+        return pl.ds(pl.multiple_of(n * group, group), group)
+
+    def slice_cols(n):
+        return pl.ds(pl.multiple_of(n * width, width), width)
+
+    def z_dev(dz):
+        return (lax.rem(z + dz, z_size) * Y_SIZE + y, me_n)
+
+    used = [0]
+    pending = []
+
+    def send(src, dst, device):
+        k = used[0]
+        used[0] += 1
+        copy = pltpu.make_async_remote_copy(
+            src_ref=src, dst_ref=dst, send_sem=send_sem.at[k], recv_sem=recv_sem.at[k],
+            device_id=device, device_id_type=MESH,
+        )
+        copy.start()
+        pending.append(copy)
+        return copy
+
+    own_x = pltpu.make_async_copy(
+        x_hbm.at[group_rows(me_n), :], fg.at[me_b, :, slice_cols(me_n)], local_sem.at[0]
+    )
+    own_wn = pltpu.make_async_copy(wn_hbm, weights.at[0, slice_cols(me_n), :], local_sem.at[1])
+    own_wr = pltpu.make_async_copy(wr_hbm, weights.at[1, slice_cols(me_n), :], local_sem.at[2])
+    tile_copy = pltpu.make_async_copy(t_hbm.at[0, 0], tiles, local_sem.at[3])
+    ow_copy = pltpu.make_async_copy(ow_hbm, ow, local_sem.at[4])
+    cot_copy = pltpu.make_async_copy(cot_hbm, cot, local_sem.at[5])
+    x_copy = pltpu.make_async_copy(x_hbm, x_vm, local_sem.at[6])
+    for copy in (own_x, tile_copy, cot_copy, ow_copy, own_wn, own_wr, x_copy):
+        copy.start()
+
+    barrier = pltpu.get_barrier_semaphore()
+    partners = [(me_b, n) for n in (core_n, x_n, xc_n)]
+    partners += [z_dev(dz) for dz in range(1, z_size)] + [y_dev]
+    for device in partners:
+        pl.semaphore_signal(barrier, inc=1, device_id=device, device_id_type=MESH)
+    pl.semaphore_wait(barrier, len(partners))
+
+    narrow_partners = (xc_n, x_n, core_n)
+    first = [
+        send(x_hbm.at[group_rows(n), :], fg.at[me_b, :, slice_cols(me_n)], (me_b, n))
+        for n in narrow_partners
+    ]
+    own_x.wait()
+    for copy in first:
+        copy.wait_recv()
+    z_order = sorted(range(1, z_size), key=lambda dz: abs(dz - z_size / 2))
+    blocks = {dz: send(fg.at[me_b], fg.at[me_b], z_dev(dz)) for dz in z_order}
+    from_y_blocks = [send(fg.at[me_b], fg.at[me_b], y_dev)]
+    w_core = [
+        send(w, weights.at[i, slice_cols(me_n), :], (me_b, core_n))
+        for i, w in enumerate((wn_hbm, wr_hbm))
+    ]
+    w_x = [
+        send(w, weights.at[i, slice_cols(me_n), :], (me_b, x_n))
+        for i, w in enumerate((wn_hbm, wr_hbm))
+    ]
+
+    tile_copy.wait()
+    live = count_ref[0, 0]
+    chunk = 32
+    positions = dense.shape[0] // side * (dense.shape[1] // side)
+    across = dense.shape[1] // side
+
+    def densify(step, _):
+        at = pl.ds(pl.multiple_of(step * chunk, chunk), chunk)
+
+        def add_slot(s, sums):
+            tile = tiles[s, at, :].astype(f32)
+            place = rows_ref[0, 0, s] * across + cols_ref[0, 0, s]
+            place = jnp.where(s < live, place, -1)
+            return tuple(
+                sums[p] + tile * jnp.where(place == p, 1.0, 0.0).astype(f32)
+                for p in range(positions)
+            )
+
+        sums = lax.fori_loop(
+            0, slots, add_slot, tuple(jnp.zeros((chunk, side), f32) for _ in range(positions))
+        )
+        for p in range(positions):
+            row = pl.ds(pl.multiple_of(p // across * side + step * chunk, chunk), chunk)
+            dense[row, pl.ds(p % across * side, side)] = sums[p].astype(bf16)
+        return 0
+
+    lax.fori_loop(0, side // chunk, densify, 0)
+
+    for dz in z_order:
+        blocks[dz].wait_recv()
+        b = lax.rem(z + z_size - dz, z_size) * Y_SIZE + y
+        from_y_blocks.append(send(fg.at[b], fg.at[b], y_dev))
+    w_fwd = []
+    for i in range(2):
+        w_x[i].wait_recv()
+        w_fwd.append(
+            send(
+                weights.at[i, slice_cols(x_n), :], weights.at[i, slice_cols(x_n), :],
+                (me_b, core_n),
+            )
+        )
+    cot_copy.wait()
+    ow_copy.wait()
+    hidden_grad = lax.dot_general(
+        cot[group_rows(me_n), :], ow[...], (((1,), (1,)), ((), ())), preferred_element_type=f32
+    )
+    for copy in from_y_blocks:
+        copy.wait_recv()
+    part[...] = jnp.dot(
+        dense[...], fg[...].reshape(wide * group, hidden_width), preferred_element_type=f32
+    )
+    part_bf[...] = part[...].astype(bf16)
+    arriving = [
+        send(part_bf.at[group_rows(n), :], agg_in.at[i], (me_b, n))
+        for i, n in enumerate(narrow_partners)
+    ]
+    own_wn.wait()
+    own_wr.wait()
+    for copy in w_core + w_fwd:
+        copy.wait_recv()
+    pre = jnp.dot(fg[me_b], weights[1], preferred_element_type=f32)
+    agg32 = part[group_rows(me_n), :]
+    for i, copy in enumerate(arriving):
+        copy.wait_recv()
+        agg32 = agg32 + agg_in[i].astype(f32)
+    agg_r[...] = agg32.astype(bf16)
+    agg_moves = [
+        send(agg_r.at[:, slice_cols(n)], agg_cols.at[group_rows(me_n), :], (me_b, n))
+        for n in narrow_partners
+    ]
+    pre = pre + jnp.dot(agg_r[...], weights[0], preferred_element_type=f32)
+    sig = jax.nn.sigmoid(pre)
+    mine = group_rows(me_n)
+    pg[mine, :] = (hidden_grad * sig * (1.0 + pre * (1.0 - sig))).astype(bf16)
+    hid[mine, :] = (pre * sig).astype(bf16)
+    pg_x = send(pg.at[mine, :], pg.at[mine, :], (me_b, x_n))
+    hid_x = send(hid.at[mine, :], hid.at[mine, :], (me_b, x_n))
+    pg_core = [send(pg.at[mine, :], pg.at[mine, :], (me_b, core_n))]
+    hid_core = [send(hid.at[mine, :], hid.at[mine, :], (me_b, core_n))]
+    agg_cols[mine, :] = agg_r[:, slice_cols(me_n)]
+    theirs = group_rows(x_n)
+    pg_x.wait_recv()
+    pg_core.append(send(pg.at[theirs, :], pg.at[theirs, :], (me_b, core_n)))
+    hid_x.wait_recv()
+    hid_core.append(send(hid.at[theirs, :], hid.at[theirs, :], (me_b, core_n)))
+
+    x_copy.wait()
+    for copy in agg_moves + pg_core:
+        copy.wait_recv()
+    contract_rows = (((0,), (0,)), ((), ()))
+    grad32[pl.ds(0, width), :] = lax.dot_general(
+        agg_cols[...], pg[...], contract_rows, preferred_element_type=f32
+    )
+    grad32[pl.ds(width, width), :] = lax.dot_general(
+        x_vm[...], pg[...], contract_rows, preferred_element_type=f32
+    )
+    for copy in hid_core:
+        copy.wait_recv()
+    grad32[pl.ds(2 * width, width), :] = lax.dot_general(
+        cot[:, slice_cols(me_n)], hid[...], contract_rows, preferred_element_type=f32
+    )
+    grad[...] = grad32[...].astype(bf16)
+
+    def piece_rows(b):
+        return pl.ds(pl.multiple_of(b * piece, 16), piece)
+
+    def z_at(dz):
+        return lax.rem(z + dz, z_size)
+
+    halves = [
+        send(grad.at[piece_rows(z_at(dz) * Y_SIZE + other_y), :], from_y.at[dz], y_dev)
+        for dz in z_order + [0]
+    ]
+    arriving_z = []
+    for dz, copy in zip(z_order + [0], halves):
+        copy.wait_recv()
+        both = grad32[piece_rows(z_at(dz) * Y_SIZE + y), :] + from_y[dz].astype(f32)
+        if dz:
+            to_z[dz] = both.astype(bf16)
+            arriving_z.append((dz, send(to_z.at[dz], from_z.at[dz], z_dev(dz))))
+    lo[...] = jnp.dot(hid[...], ow[:, slice_cols(me_n)], preferred_element_type=f32)
+    lo_copy = pltpu.make_async_copy(lo, lo_out, local_sem.at[7])
+    lo_copy.start()
+    for dz, copy in arriving_z:
+        copy.wait_recv()
+        both = both + from_z[dz].astype(f32)
+    gall[me_b] = both.astype(bf16)
+    done = {dz: send(gall.at[me_b], gall.at[me_b], z_dev(dz)) for dz in z_order}
+    last = [send(gall.at[me_b], gall.at[me_b], y_dev)]
+    for dz in z_order:
+        done[dz].wait_recv()
+        b = lax.rem(z + z_size - dz, z_size) * Y_SIZE + y
+        last.append(send(gall.at[b], gall.at[b], y_dev))
+    for copy in last:
+        copy.wait_recv()
+    out_copy = pltpu.make_async_copy(gall, grads_out, local_sem.at[8])
+    out_copy.start()
+    for copy in pending:
+        copy.wait_send()
+    lo_copy.wait()
+    out_copy.wait()
+
+
+def per_device_fused(
+    wide, narrow,
+    features, tile_blocks, tile_rows, tile_cols, tile_count,
+    neighbor_weight, root_weight, output_weight, cotangent,
+):
+    node_rows, width = features.shape
+    hidden_width = output_weight.shape[0]
+    group = node_rows // narrow
+    side = tile_blocks.shape[-1]
+    z_size = wide // Y_SIZE
+    piece = 3 * width // wide
+    bf16, f32 = jnp.bfloat16, jnp.float32
+    copies = 11 + 3 * (z_size + z_size) + 12 + z_size + 3
+    hbm = pl.BlockSpec(memory_space=pl.ANY)
+    smem = pl.BlockSpec(memory_space=pltpu.SMEM)
+    grads, product = pl.pallas_call(
+        functools.partial(fused_kernel, wide, narrow),
+        out_shape=(
+            jax.ShapeDtypeStruct((wide, piece, hidden_width), bf16),
+            jax.ShapeDtypeStruct((node_rows, width), f32),
+        ),
+        in_specs=[hbm, hbm, smem, smem, smem, hbm, hbm, hbm, hbm],
+        out_specs=(hbm, hbm),
+        scratch_shapes=[
+            pltpu.VMEM((node_rows, width), bf16),
+            pltpu.VMEM(tile_blocks.shape[2:], bf16),
+            pltpu.VMEM((hidden_width, hidden_width), bf16),
+            pltpu.VMEM((node_rows, hidden_width), bf16),
+            pltpu.VMEM((wide, group, hidden_width), bf16),
+            pltpu.VMEM((2, hidden_width, hidden_width), bf16),
+            pltpu.VMEM((node_rows, wide * group), bf16),
+            pltpu.VMEM((node_rows, hidden_width), f32),
+            pltpu.VMEM((node_rows, hidden_width), bf16),
+            pltpu.VMEM((narrow - 1, group, hidden_width), bf16),
+            pltpu.VMEM((group, hidden_width), bf16),
+            pltpu.VMEM((node_rows, width), bf16),
+            pltpu.VMEM((node_rows, hidden_width), bf16),
+            pltpu.VMEM((node_rows, hidden_width), bf16),
+            pltpu.VMEM((3 * width, hidden_width), f32),
+            pltpu.VMEM((3 * width, hidden_width), bf16),
+            pltpu.VMEM((z_size, piece, hidden_width), bf16),
+            pltpu.VMEM((z_size, piece, hidden_width), bf16),
+            pltpu.VMEM((z_size, piece, hidden_width), bf16),
+            pltpu.VMEM((wide, piece, hidden_width), bf16),
+            pltpu.VMEM((node_rows, width), f32),
+            pltpu.SemaphoreType.DMA((9,)),
+            pltpu.SemaphoreType.DMA((copies,)),
+            pltpu.SemaphoreType.DMA((copies,)),
+        ],
+        compiler_params=pltpu.CompilerParams(
+            collective_id=0, has_side_effects=True, vmem_limit_bytes=40 * 1024 * 1024
+        ),
+    )(
+        features, tile_blocks, tile_rows, tile_cols, tile_count,
+        neighbor_weight, root_weight, output_weight, cotangent,
+    )
+    grads = grads.reshape(3 * width, hidden_width)
+    layer_output = (features.astype(f32) + product).astype(bf16)
+    return (
+        layer_output,
+        grads[:width].astype(f32),
+        grads[width : 2 * width].astype(f32),
+        grads[2 * width :].T.astype(f32),
+    )
+
+
 def solution(mesh):
+    wide, narrow = mesh.shape["wide"], mesh.shape["narrow"]
+    if wide == 8 and narrow == 4:
+        per_device = functools.partial(per_device_fused, wide, narrow)
+    else:
+        per_device = per_device_large
     return jax.shard_map(
         per_device,
         mesh=mesh,

time: 223 us -> 62.5 us (0.28); the launches traced: 220 us -> 62.2 us
  waiting for transfers between devices: 106 us -> 0 us
  Pallas kernels: 0 us -> 51.2 us
  blocking collectives: 48.1 us -> 0 us
  matrix products: 21.2 us -> 0 us
  between operations: 17.4 us -> 1.31 us
  local copies, waits for them, and re-layouts: 19.8 us -> 7.46 us
  other arithmetic: 7.97 us -> 2.21 us
    psum x2 -> x0, waiting for transfers between devices: 105 us -> none  [the longest x1 74.5 us: per_device(): lax.psum((neighbor_part, root_part, output_part), 'wide')]
    pallas_call x0 -> x1, Pallas kernels: none -> 51.2 us  [per_device_fused(): pl.pallas_call(functools.partial(fused_kernel, wide, narrow), out_shape=(...]
    all_gather x3 -> x0, blocking collectives: 41.7 us -> none  [the longest x1 31.7 us: per_device(): columns = lax.all_gather(features, 'wide', axis=0, tiled=True)]
    dot_general x19 -> x0, matrix products: 21.2 us -> none  [the longest x6 7.85 us: one_turn(): jnp.einsum('tij,tjh->tih', some_tiles, picked, preferred_element_type=jnp...]
    squeeze x3 -> x0, local copies, waits for them, and re-layouts: 7.79 us -> none  [the longest x1 6.61 us: per_device(): all_tiles[0, source]]
    unnamed x1 -> x0, blocking collectives: 6.39 us -> none
    gather x6 -> x0, local copies, waits for them, and re-layouts: 4.18 us -> none  [one_turn(): picked = column_tiles[some_cols]]
    select_n x6 -> x0, other arithmetic: 3.77 us -> none  [one_turn(): picked = column_tiles[some_cols]]
  transfers between devices with their start and end apart: 3 -> 0, of which waited for: 2 -> 0; matrix products, arithmetic and copies ran while one was open for 2% -> 0% of each run, Pallas kernels for 0% -> 0%
where the time goes in v1:
time: 62.5 us; the launch traced here: 62.2 us
  Pallas kernels  51.2 us (82%)
  local copies, waits for them, and re-layouts  7.46 us (12%)
  other arithmetic  2.21 us (4%)
  between operations  1.31 us (2%)
    pallas_call x1, Pallas kernels, per_device_fused(): pl.pallas_call(functools.partial(fused_kernel, wide, narrow), out_shape=(...  51.2 us
    unnamed x17, local copies, waits for them, and re-layouts  7.46 us

profile of v1, /device:TPU:0, one launch (start us, length us, event | category | flops | bytes accessed | tf_op | source)
XLA Modules:
  0.0 62.2 jit_solution(74845425271368398)
XLA Ops:
  1.3 0.0 copy-start
  1.3 1.4 %copy-done = bf16[1,1,48,128,128]{4,3,2,1,0:T(8,128)(2,1)S(1)} copy-done((bf16[1,1,48,128,128]{4,3,2,1,0:T(8,128)(2,1)S(1)}, bf16[1,1,48,128,128]{4,3,2,1,0:T(8,128)(2,1)}, u32[]{:S(2)}) %copy-start) | copy-done | bytes 1572888
  2.7 0.0 copy-start.1
  2.7 1.0 %copy-done.1 = bf16[512,512]{1,0:T(8,128)(2,1)S(1)} copy-done((bf16[512,512]{1,0:T(8,128)(2,1)S(1)}, bf16[512,512]{1,0:T(8,128)(2,1)}, u32[]{:S(2)}) %copy-start.1) | copy-done | bytes 524312
  3.7 0.0 copy-start.2
  3.7 0.8 %copy-done.2 = bf16[256,128]{1,0:T(8,128)(2,1)S(1)} copy-done((bf16[256,128]{1,0:T(8,128)(2,1)S(1)}, bf16[256,128]{1,0:T(8,128)(2,1)}, u32[]{:S(2)}) %copy-start.2) | copy-done | bytes 65560
  4.6 0.0 copy-start.3
  4.6 0.9 %copy-done.3 = bf16[256,512]{1,0:T(8,128)(2,1)S(1)} copy-done((bf16[256,512]{1,0:T(8,128)(2,1)S(1)}, bf16[256,512]{1,0:T(8,128)(2,1)}, u32[]{:S(2)}) %copy-start.3) | copy-done | bytes 262168
  5.5 0.0 copy-start.4
  5.5 0.9 %copy-done.4 = bf16[128,512]{1,0:T(8,128)(2,1)S(1)} copy-done((bf16[128,512]{1,0:T(8,128)(2,1)S(1)}, bf16[128,512]{1,0:T(8,128)(2,1)}, u32[]{:S(2)}) %copy-start.4) | copy-done | bytes 131096
  6.4 0.0 copy-start.5
  6.4 0.9 %copy-done.5 = bf16[128,512]{1,0:T(8,128)(2,1)S(1)} copy-done((bf16[128,512]{1,0:T(8,128)(2,1)S(1)}, bf16[128,512]{1,0:T(8,128)(2,1)}, u32[]{:S(2)}) %copy-start.5) | copy-done | bytes 131096
  7.3 0.0 copy-start.6
  7.3 0.7 %copy-done.6 = s32[1,1,48]{2,1,0:T(1,128)S(1)} copy-done((s32[1,1,48]{2,1,0:T(1,128)S(1)}, s32[1,1,48]{2,1,0:T(1,128)}, u32[]{:S(2)}) %copy-start.6) | copy-done | bytes 216
  8.0 0.0 copy-start.7
  8.0 0.7 %copy-done.7 = s32[1,1,48]{2,1,0:T(1,128)S(1)} copy-done((s32[1,1,48]{2,1,0:T(1,128)S(1)}, s32[1,1,48]{2,1,0:T(1,128)}, u32[]{:S(2)}) %copy-start.7) | copy-done | bytes 216
  8.6 51.2 %shard_map.120 = (bf16[8,48,512]{2,1,0:T(8,128)(2,1)S(1)}, f32[256,128]{1,0:T(8,128)S(1)}) custom-call(bf16[256,128]{1,0:T(8,128)(2,1)S(1)} %copy-done.2, bf16[1,1,48,128,128]{4,3,2,1,0:T(8,128)(2,1)S(1)} %copy-done, s32[1,1,48]{2,1,0:T(1,128)S(1)} %copy-done.6, s32[1,1,48]{2,1,0:T(1,128)S(1)} %copy-done.7, s32[1,1]{1,0:T(1,128)S(6)} %copy.15.count_ref, ...), custom_call_target="tpu_custom_call" | custom-call | tf_op jit(solution)/shard_map/pallas_call | solution.py:354
  59.9 0.6 %add_convert_fusion = bf16[256,128]{1,0:T(8,128)(2,1)} fusion(f32[256,128]{1,0:T(8,128)S(1)} %get-tuple-element.6, bf16[256,128]{1,0:T(8,128)(2,1)S(1)} %copy-done.2), kind=kLoop, calls=%fused_computation.3 | loop fusion | flops 98304 | bytes 262144 | tf_op jit(solution)/shard_map/convert_element_type | solution.py:396
  60.5 0.8 %fusion = (bf16[128,512]{1,0:T(8,128)(2,1)S(1)}, f32[128,512]{1,0:T(8,128)}, f32[128,512]{1,0:T(8,128)}) fusion(bf16[384,512]{1,0:T(8,128)(2,1)S(1)} %bitcast.3), kind=kLoop, calls=%fused_computation.4 | loop fusion | flops 131072 | bytes 1048576 | tf_op jit(solution)/shard_map/slice | solution.py:401
  61.3 0.1 copy.14
  61.5 0.7 %convert_bitcast_fusion = f32[512,128]{1,0:T(8,128)} fusion(bf16[128,512]{0,1:T(8,128)(2,1)S(1)} %copy.14), kind=kLoop, calls=%fused_computation | loop fusion | flops 65536 | bytes 393216 | tf_op jit(solution)/shard_map/convert_element_type | solution.py:401
Async XLA Ops:
  1.3 1.4 %copy-start = (bf16[1,1,48,128,128]{4,3,2,1,0:T(8,128)(2,1)S(1)}, bf16[1,1,48,128,128]{4,3,2,1,0:T(8,128)(2,1)}, u32[]{:S(2)}) copy-start(bf16[1,1,48,128,128]{4,3,2,1,0:T(8,128)(2,1)} %t_hbm.1) | copy-start | bytes 4718596
  2.7 1.0 %copy-start.1 = (bf16[512,512]{1,0:T(8,128)(2,1)S(1)}, bf16[512,512]{1,0:T(8,128)(2,1)}, u32[]{:S(2)}) copy-start(bf16[512,512]{1,0:T(8,128)(2,1)} %ow_hbm.1) | copy-start | bytes 1572868
  3.7 0.8 %copy-start.2 = (bf16[256,128]{1,0:T(8,128)(2,1)S(1)}, bf16[256,128]{1,0:T(8,128)(2,1)}, u32[]{:S(2)}) copy-start(bf16[256,128]{1,0:T(8,128)(2,1)} %x_hbm.1) | copy-start | bytes 196612
  4.6 0.9 %copy-start.3 = (bf16[256,512]{1,0:T(8,128)(2,1)S(1)}, bf16[256,512]{1,0:T(8,128)(2,1)}, u32[]{:S(2)}) copy-start(bf16[256,512]{1,0:T(8,128)(2,1)} %cot_hbm.1) | copy-start | bytes 786436
  5.5 0.9 %copy-start.4 = (bf16[128,512]{1,0:T(8,128)(2,1)S(1)}, bf16[128,512]{1,0:T(8,128)(2,1)}, u32[]{:S(2)}) copy-start(bf16[128,512]{1,0:T(8,128)(2,1)} %wn_hbm.1) | copy-start | bytes 393220
  6.4 0.9 %copy-start.5 = (bf16[128,512]{1,0:T(8,128)(2,1)S(1)}, bf16[128,512]{1,0:T(8,128)(2,1)}, u32[]{:S(2)}) copy-start(bf16[128,512]{1,0:T(8,128)(2,1)} %wr_hbm.1) | copy-start | bytes 393220
  7.3 0.7 %copy-start.6 = (s32[1,1,48]{2,1,0:T(1,128)S(1)}, s32[1,1,48]{2,1,0:T(1,128)}, u32[]{:S(2)}) copy-start(s32[1,1,48]{2,1,0:T(1,128)} %rows_ref.1) | copy-start | bytes 580
  8.0 0.7 %copy-start.7 = (s32[1,1,48]{2,1,0:T(1,128)S(1)}, s32[1,1,48]{2,1,0:T(1,128)}, u32[]{:S(2)}) copy-start(s32[1,1,48]{2,1,0:T(1,128)} %cols_ref.1) | copy-start | bytes 580

commit v2 on v1

v2 whole, which is shorter than its diff:
```python
import functools
import math

import jax
import jax.numpy as jnp
from jax import lax
from jax.experimental import pallas as pl
from jax.experimental.pallas import tpu as pltpu
from jax.sharding import PartitionSpec as P


def tile_sum(block_tiles, row_ids, col_ids, live_count, column_tiles, tile_rows_count):
    capacity = block_tiles.shape[0]
    block_size = math.gcd(capacity, 24)
    tile_side = block_tiles.shape[-1]
    feature_width = column_tiles.shape[-1]
    row_range = jnp.arange(tile_rows_count, dtype=jnp.int32)
    slot_range = jnp.arange(block_size, dtype=jnp.int32)

    def one_turn(turn_index, running):
        first_slot = turn_index * block_size
        some_tiles = lax.dynamic_slice_in_dim(block_tiles, first_slot, block_size, 0)
        some_rows = lax.dynamic_slice_in_dim(row_ids, first_slot, block_size, 0)
        some_cols = lax.dynamic_slice_in_dim(col_ids, first_slot, block_size, 0)
        picked = column_tiles[some_cols]
        product = jnp.einsum("tij,tjh->tih", some_tiles, picked, preferred_element_type=jnp.float32)
        alive = (first_slot + slot_range < live_count).astype(jnp.float32)
        placing = alive[:, None] * (some_rows[:, None] == row_range[None, :]).astype(jnp.float32)
        return running + jnp.einsum("tr,tih->rih", placing, product)

    block_turns = (live_count + block_size - 1) // block_size
    start_value = jnp.zeros((tile_rows_count, tile_side, feature_width), jnp.float32)
    summed = lax.fori_loop(0, block_turns, one_turn, start_value)
    return summed.reshape(tile_rows_count * tile_side, feature_width)


def per_device_large(
    features,
    tile_blocks,
    tile_rows,
    tile_cols,
    tile_count,
    neighbor_weight,
    root_weight,
    output_weight,
    cotangent,
):
    node_rows = features.shape[0]
    slice_width = features.shape[1]
    wide_count = lax.axis_size("wide")
    narrow_count = lax.axis_size("narrow")
    tile_side = tile_blocks.shape[-1]
    tile_rows_count = node_rows // tile_side
    group_rows = node_rows // narrow_count
    all_tiles, all_rows, all_cols, all_counts = (
        lax.all_gather(tile_blocks, "narrow", axis=1, tiled=True),
        lax.all_gather(tile_rows, "narrow", axis=1, tiled=True),
        lax.all_gather(tile_cols, "narrow", axis=1, tiled=True),
        lax.all_gather(tile_count, "narrow", axis=1, tiled=True),
    )
    columns = lax.all_gather(features, "wide", axis=0, tiled=True)
    groups = columns.reshape(wide_count, narrow_count, group_rows, slice_width).transpose(
        1, 0, 2, 3
    )
    groups = groups.reshape(narrow_count, -1, tile_side, slice_width)
    running = jnp.zeros((node_rows, slice_width), jnp.float32)
    for source in range(narrow_count):
        running = running + tile_sum(
            all_tiles[0, source],
            all_rows[0, source],
            all_cols[0, source],
            all_counts[0, source],
            groups[source],
            tile_rows_count,
        )
    agg = running.astype(jnp.bfloat16)
    partial_pre = jnp.dot(agg, neighbor_weight, preferred_element_type=jnp.float32) + jnp.dot(
        features, root_weight, preferred_element_type=jnp.float32
    )
    pre = lax.psum(partial_pre, "narrow")
    hidden = jax.nn.silu(pre).astype(jnp.bfloat16)
    narrow_index = lax.axis_index("narrow")
    out_columns = lax.dynamic_slice_in_dim(
        output_weight, narrow_index * slice_width, slice_width, 1
    )
    layer_output = (
        features.astype(jnp.float32)
        + jnp.dot(hidden, out_columns, preferred_element_type=jnp.float32)
    ).astype(jnp.bfloat16)
    hidden_grad = jnp.dot(cotangent, output_weight.T, preferred_element_type=jnp.float32)
    sigmoid_pre = jax.nn.sigmoid(pre)
    pre_grad = (hidden_grad * sigmoid_pre * (1.0 + pre * (1.0 - sigmoid_pre))).astype(jnp.bfloat16)
    cot_columns = lax.dynamic_slice_in_dim(cotangent, narrow_index * slice_width, slice_width, 1)
    neighbor_part = jnp.dot(agg.T, pre_grad, preferred_element_type=jnp.float32)
    root_part = jnp.dot(features.T, pre_grad, preferred_element_type=jnp.float32)
    output_part = jnp.dot(hidden.T, cot_columns, preferred_element_type=jnp.float32)
    neighbor_grad, root_grad, output_grad = lax.psum(
        (neighbor_part, root_part, output_part), "wide"
    )
    return (layer_output, neighbor_grad, root_grad, output_grad)


Y_SIZE = 2
CORES = 2
MESH = pl.DeviceIdType.MESH


def fused_kernel(
    wide, narrow,
    x_hbm, t_hbm, rows_ref, cols_ref, count_ref, wn_hbm, wr_hbm, ow_hbm, cot_hbm,
    grads_out, lo_out,
    xf, tiles, ow, cot, wn, wr, dense, part, part_bf, pre_in, agg,
    pg, hid, grad32, grad, from_y, to_z, from_z, gall, lo,
    local_sem, send_sem, recv_sem,
):
    z_size = wide // Y_SIZE
    me_b = lax.axis_index("wide")
    me_n = lax.axis_index("narrow")
    z, y = me_b // Y_SIZE, me_b % Y_SIZE
    other_y = 1 - y
    core_n = me_n // CORES * CORES + (1 - me_n % CORES)
    x_n = (me_n + CORES) % narrow
    xc_n = (core_n + CORES) % narrow
    node_rows, width = x_hbm.shape
    hidden_width = ow_hbm.shape[0]
    group = node_rows // narrow
    side = t_hbm.shape[-1]
    slots = t_hbm.shape[2]
    piece = width // wide
    tile_rows_count = node_rows // side
    across = dense.shape[-1] // side
    f32, bf16 = jnp.float32, jnp.bfloat16
    y_dev = (z * Y_SIZE + other_y, me_n)

    def group_rows(n):
        return pl.ds(pl.multiple_of(n * group, group), group)

    def slice_cols(n):
        return pl.ds(pl.multiple_of(n * width, width), width)

    def z_at(dz):
        return lax.rem(z + dz, z_size)

    def z_dev(dz):
        return (z_at(dz) * Y_SIZE + y, me_n)

    def z_source(dz):
        return lax.rem(z + z_size - dz, z_size) * Y_SIZE + y

    used = [0]
    pending = []

    def send(src, dst, device):
        k = used[0]
        used[0] += 1
        copy = pltpu.make_async_remote_copy(
            src_ref=src, dst_ref=dst, send_sem=send_sem.at[k], recv_sem=recv_sem.at[k],
            device_id=device, device_id_type=MESH,
        )
        copy.start()
        pending.append(copy)
        return copy

    barrier = pltpu.get_barrier_semaphore()
    partners = [(me_b, n) for n in (core_n, x_n, xc_n)]
    partners += [z_dev(dz) for dz in range(1, z_size)] + [y_dev]
    for device in partners:
        pl.semaphore_signal(barrier, inc=1, device_id=device, device_id_type=MESH)

    local = [
        pltpu.make_async_copy(src, dst, local_sem.at[k])
        for k, (src, dst) in enumerate(
            (
                (t_hbm.at[0, 0], tiles),
                (x_hbm, xf.at[me_b]),
                (wr_hbm, wr),
                (wn_hbm, wn),
                (cot_hbm, cot),
                (ow_hbm, ow),
            )
        )
    ]
    for copy in local:
        copy.start()
    tile_copy, x_copy, wr_copy, wn_copy, cot_copy, ow_copy = local

    live = count_ref[0, 0]
    chunk = 32
    positions = tile_rows_count * across
    steps = side // chunk

    def densify(step, _):
        at = pl.ds(pl.multiple_of(step * chunk, chunk), chunk)

        def add_slot(s, sums):
            tile = tiles[s, at, :].astype(f32)
            place = rows_ref[0, 0, s] * across + cols_ref[0, 0, s]
            place = jnp.where(s < live, place, -1)
            return tuple(
                sums[p] + tile * jnp.where(place == p, 1.0, 0.0).astype(f32)
                for p in range(positions)
            )

        sums = lax.fori_loop(
            0, slots, add_slot, tuple(jnp.zeros((chunk, side), f32) for _ in range(positions))
        )
        for p in range(positions):
            dense[me_n, p // across, at, pl.ds(p % across * side, side)] = sums[p].astype(bf16)
        return 0

    def half(n, h):
        return dense.at[n, :, pl.ds(h * (side // 2), side // 2), :]

    tile_copy.wait()
    lax.fori_loop(0, steps // 2, densify, 0)
    pl.semaphore_wait(barrier, len(partners))

    z_order = sorted(range(1, z_size), key=lambda dz: abs(dz - z_size / 2))
    blocks = {dz: send(x_hbm, xf.at[me_b], z_dev(dz)) for dz in z_order}
    y_blocks = [send(x_hbm, xf.at[me_b], y_dev)]
    dense_x = [send(half(me_n, 0), half(me_n, 0), (me_b, x_n))]
    dense_core = [send(half(me_n, 0), half(me_n, 0), (me_b, core_n))]
    lax.fori_loop(steps // 2, steps, densify, 0)
    dense_x.append(send(half(me_n, 1), half(me_n, 1), (me_b, x_n)))
    dense_core.append(send(half(me_n, 1), half(me_n, 1), (me_b, core_n)))
    dense_fwd = []

    def pass_block(dz):
        blocks[dz].wait_recv()
        b = z_source(dz)
        y_blocks.append(send(xf.at[b], xf.at[b], y_dev))

    def pass_half(h):
        dense_x[h].wait_recv()
        dense_fwd.append(send(half(x_n, h), half(x_n, h), (me_b, core_n)))

    for dz in z_order[1:]:
        pass_block(dz)
    pass_half(0)
    pass_block(z_order[0])
    cot_copy.wait()
    ow_copy.wait()
    hidden_grad = lax.dot_general(
        cot[group_rows(me_n), :], ow[...], (((1,), (1,)), ((), ())), preferred_element_type=f32
    )
    pass_half(1)
    x_copy.wait()
    wr_copy.wait()
    wn_copy.wait()
    part[...] = jnp.dot(xf[me_b], wr[...], preferred_element_type=f32)

    for copy in y_blocks:
        copy.wait_recv()

    def product(n):
        column_tiles = xf[:, group_rows(n), :].reshape(wide * group, width)
        return jnp.dot(
            dense[n].reshape(node_rows, wide * group), column_tiles, preferred_element_type=f32
        )

    total = product(me_n)
    for copy in dense_core:
        copy.wait_recv()
    total = total + product(core_n)
    total = total + product(x_n)
    for copy in dense_fwd:
        copy.wait_recv()
    total = total + product(xc_n)
    agg[...] = total.astype(bf16)

    arriving = []
    narrow_partners = (xc_n, x_n, core_n)
    for i, n in enumerate(narrow_partners):
        at = group_rows(n)
        there = part[at, :] + jnp.dot(agg[at, :], wn[...], preferred_element_type=f32)
        part_bf[i] = there.astype(bf16)
        arriving.append(send(part_bf.at[i], pre_in.at[i], (me_b, n)))
    mine = group_rows(me_n)
    pre = part[mine, :] + jnp.dot(agg[mine, :], wn[...], preferred_element_type=f32)
    for i, copy in enumerate(arriving):
        copy.wait_recv()
        pre = pre + pre_in[i].astype(f32)
    sig = jax.nn.sigmoid(pre)
    pg[mine, :] = (hidden_grad * sig * (1.0 + pre * (1.0 - sig))).astype(bf16)
    pg_x = send(pg.at[mine, :], pg.at[mine, :], (me_b, x_n))
    pg_core = [send(pg.at[mine, :], pg.at[mine, :], (me_b, core_n))]
    hid[mine, :] = (pre * sig).astype(bf16)
    hid_x = send(hid.at[mine, :], hid.at[mine, :], (me_b, x_n))
    hid_core = [send(hid.at[mine, :], hid.at[mine, :], (me_b, core_n))]
    theirs = group_rows(x_n)
    pg_x.wait_recv()
    pg_core.append(send(pg.at[theirs, :], pg.at[theirs, :], (me_b, core_n)))
    hid_x.wait_recv()
    hid_core.append(send(hid.at[theirs, :], hid.at[theirs, :], (me_b, core_n)))
    for copy in pg_core:
        copy.wait_recv()

    contract_rows = (((0,), (0,)), ((), ()))
    tracks = (pl.ds(0, 2), pl.ds(2, 1))

    def piece_of(track, b):
        return (tracks[track], pl.ds(pl.multiple_of(b * piece, piece), piece), slice(None))

    def fill(k, left, right):
        value = lax.dot_general(left, right, contract_rows, preferred_element_type=f32)
        grad32[k] = value
        grad[k] = value.astype(bf16)

    def to_other_y(track):
        return [
            send(
                grad.at[piece_of(track, z_at(dz) * Y_SIZE + other_y)],
                from_y.at[dz, tracks[track]],
                y_dev,
            )
            for dz in z_order + [0]
        ]

    fill(0, agg[...], pg[...])
    fill(1, xf[me_b], pg[...])
    halves = [to_other_y(0)]
    for copy in hid_core:
        copy.wait_recv()
    fill(2, cot[:, slice_cols(me_n)], hid[...])
    halves.append(to_other_y(1))

    sums, arriving_z = [], []
    for track in range(2):
        along = tracks[track]
        arriving_z.append([])
        for dz, copy in zip(z_order + [0], halves[track]):
            copy.wait_recv()
            both = grad32[piece_of(track, z_at(dz) * Y_SIZE + y)] + from_y[dz, along].astype(f32)
            if dz:
                to_z[dz, along] = both.astype(bf16)
                arriving_z[track].append(
                    (dz, send(to_z.at[dz, along], from_z.at[dz, along], z_dev(dz)))
                )
        sums.append(both)
    lo[...] = jnp.dot(hid[...], ow[:, slice_cols(me_n)], preferred_element_type=f32)
    lo_copy = pltpu.make_async_copy(lo, lo_out, local_sem.at[6])
    lo_copy.start()
    last, done = [], []
    for track in range(2):
        both = sums[track]
        for dz, copy in arriving_z[track]:
            copy.wait_recv()
            both = both + from_z[dz, tracks[track]].astype(f32)
        own = piece_of(track, me_b)
        gall[own] = both.astype(bf16)
        done.append({dz: send(gall.at[own], gall.at[own], z_dev(dz)) for dz in z_order})
        last.append(send(gall.at[own], gall.at[own], y_dev))
    for track in range(2):
        for dz in z_order[1:] + z_order[:1]:
            done[track][dz].wait_recv()
            at = piece_of(track, z_source(dz))
            last.append(send(gall.at[at], gall.at[at], y_dev))
    for copy in last:
        copy.wait_recv()
    out_copy = pltpu.make_async_copy(gall, grads_out, local_sem.at[7])
    out_copy.start()
    for copy in pending:
        copy.wait_send()
    lo_copy.wait()
    out_copy.wait()


def per_device_fused(
    wide, narrow,
    features, tile_blocks, tile_rows, tile_cols, tile_count,
    neighbor_weight, root_weight, output_weight, cotangent,
):
    node_rows, width = features.shape
    hidden_width = output_weight.shape[0]
    group = node_rows // narrow
    side = tile_blocks.shape[-1]
    z_size = wide // Y_SIZE
    piece = width // wide
    bf16, f32 = jnp.bfloat16, jnp.float32
    copies = 64
    hbm = pl.BlockSpec(memory_space=pltpu.HBM)
    smem = pl.BlockSpec(memory_space=pltpu.SMEM)
    grads, product = pl.pallas_call(
        functools.partial(fused_kernel, wide, narrow),
        out_shape=(
            jax.ShapeDtypeStruct((3, width, hidden_width), bf16),
            jax.ShapeDtypeStruct((node_rows, width), f32),
        ),
        in_specs=[hbm, hbm, smem, smem, smem, hbm, hbm, hbm, hbm],
        out_specs=(hbm, hbm),
        scratch_shapes=[
            pltpu.VMEM((wide, node_rows, width), bf16),
            pltpu.VMEM(tile_blocks.shape[2:], bf16),
            pltpu.VMEM((hidden_width, hidden_width), bf16),
            pltpu.VMEM((node_rows, hidden_width), bf16),
            pltpu.VMEM((width, hidden_width), bf16),
            pltpu.VMEM((width, hidden_width), bf16),
            pltpu.VMEM((narrow, node_rows // side, side, wide * group), bf16),
            pltpu.VMEM((node_rows, hidden_width), f32),
            pltpu.VMEM((narrow - 1, group, hidden_width), bf16),
            pltpu.VMEM((narrow - 1, group, hidden_width), bf16),
            pltpu.VMEM((node_rows, width), bf16),
            pltpu.VMEM((node_rows, hidden_width), bf16),
            pltpu.VMEM((node_rows, hidden_width), bf16),
            pltpu.VMEM((3, width, hidden_width), f32),
            pltpu.VMEM((3, width, hidden_width), bf16),
            pltpu.VMEM((z_size, 3, piece, hidden_width), bf16),
            pltpu.VMEM((z_size, 3, piece, hidden_width), bf16),
            pltpu.VMEM((z_size, 3, piece, hidden_width), bf16),
            pltpu.VMEM((3, width, hidden_width), bf16),
            pltpu.VMEM((node_rows, width), f32),
            pltpu.SemaphoreType.DMA((8,)),
            pltpu.SemaphoreType.DMA((copies,)),
            pltpu.SemaphoreType.DMA((copies,)),
        ],
        compiler_params=pltpu.CompilerParams(
            collective_id=0, has_side_effects=True, vmem_limit_bytes=63 * 1024 * 1024
        ),
    )(
        features, tile_blocks, tile_rows, tile_cols, tile_count,
        neighbor_weight, root_weight, output_weight, cotangent,
    )
    layer_output = (features.astype(f32) + product).astype(bf16)
    return (
        layer_output,
        grads[0].astype(f32),
        grads[1].astype(f32),
        grads[2].T.astype(f32),
    )


def solution(mesh):
    wide, narrow = mesh.shape["wide"], mesh.shape["narrow"]
    if wide == 8 and narrow == 4:
        per_device = functools.partial(per_device_fused, wide, narrow)
    else:
        per_device = per_device_large
    return jax.shard_map(
        per_device,
        mesh=mesh,
        in_specs=(
            P("wide", "narrow"),
            P("wide", "narrow", None, None, None),
            P("wide", "narrow", None),
            P("wide", "narrow", None),
            P("wide", "narrow"),
            P("narrow", None),
            P("narrow", None),
            P(),
            P("wide", None),
        ),
        out_specs=(P("wide", "narrow"), P("narrow", None), P("narrow", None), P(None, "narrow")),
        check_vma=False,
    )
```

time: 62.5 us -> 53.9 us (0.86)
  local copies, waits for them, and re-layouts: 7.46 us -> 0.84 us
  Pallas kernels: 51.2 us -> 48 us
  other arithmetic: 2.21 us -> 3.46 us
    unnamed x17 -> x3, local copies, waits for them, and re-layouts: 7.46 us -> 0.84 us
    pallas_call x1, Pallas kernels: 51.2 us -> 48 us  [per_device_fused(): pl.pallas_call(functools.partial(fused_kernel, wide, narrow), out_shape=(...]
    convert_element_type x1, other arithmetic: 0.73 us -> 1.91 us  [per_device_fused(): grads[2].T.astype(f32)]
    convert_element_type x1, other arithmetic: 0.65 us -> 1.55 us  [per_device_fused(): layer_output = (features.astype(f32) + product).astype(bf16)]
    slice x1 -> x0, other arithmetic: 0.83 us -> none  [per_device_fused(): grads[2 * width:].T.astype(f32)]
where the time goes in v2:
time: 53.9 us; the launch traced here: 53.6 us
  Pallas kernels  48 us (89%)
  other arithmetic  3.46 us (6%)
  between operations  1.34 us (2%)
  local copies, waits for them, and re-layouts  0.84 us (2%)
    pallas_call x1, Pallas kernels, per_device_fused(): pl.pallas_call(functools.partial(fused_kernel, wide, narrow), out_shape=(...  48 us
    convert_element_type x1, other arithmetic, per_device_fused(): grads[2].T.astype(f32)  1.91 us
    convert_element_type x1, other arithmetic, per_device_fused(): layer_output = (features.astype(f32) + product).astype(bf16)  1.55 us

profile of v2, /device:TPU:0, one launch (start us, length us, event | category | flops | bytes accessed | tf_op | source)
XLA Modules:
  0.0 53.6 jit_solution(11348082517343528527)
XLA Ops:
  0.6 0.0 copy-start
  1.3 48.0 %shard_map.120 = (bf16[3,128,512]{2,1,0:T(8,128)(2,1)}, f32[256,128]{1,0:T(8,128)}) custom-call(bf16[256,128]{1,0:T(8,128)(2,1)} %x_hbm.1, bf16[1,1,48,128,128]{4,3,2,1,0:T(8,128)(2,1)} %t_hbm.1, s32[1,1,48]{2,1,0:T(1,128)} %rows_ref.1, s32[1,1,48]{2,1,0:T(1,128)} %cols_ref.1, s32[1,1]{1,0:T(1,128)S(6)} %copy.14.count_ref, bf16[128,512]{1,0:T(8,128)(2,1)} %wn_hbm.1, ...), custom_call_target="tpu_custom_call" | custom-call | tf_op jit(solution)/shard_map/pallas_call | solution.py:383
  49.3 0.0 copy-done
  49.3 1.5 %add_convert_fusion = bf16[256,128]{1,0:T(8,128)(2,1)} fusion(f32[256,128]{1,0:T(8,128)} %get-tuple-element.6, bf16[256,128]{1,0:T(8,128)(2,1)S(1)} %copy-done), kind=kLoop, calls=%fused_computation.3 | loop fusion | flops 98304 | bytes 262144 | tf_op jit(solution)/shard_map/convert_element_type | solution.py:423
  50.9 1.9 %convert_bitcast_fusion = (f32[512,128]{0,1:T(8,128)S(1)}, f32[128,512]{1,0:T(8,128)}, f32[128,512]{1,0:T(8,128)}) fusion(bf16[3,128,512]{2,1,0:T(8,128)(2,1)} %get-tuple-element.7), kind=kLoop, calls=%fused_computation | loop fusion | flops 196608 | bytes 1179648 | tf_op jit(solution)/shard_map/convert_element_type | solution.py:428
  52.8 0.8 %copy.13 = f32[512,128]{1,0:T(8,128)} copy(f32[512,128]{0,1:T(8,128)S(1)} %get-tuple-element.12) | data formatting | bytes 524288
Async XLA Ops:
  0.6 48.7 %copy-start = (bf16[256,128]{1,0:T(8,128)(2,1)S(1)}, bf16[256,128]{1,0:T(8,128)(2,1)}, u32[]{:S(2)}) copy-start(bf16[256,128]{1,0:T(8,128)(2,1)} %x_hbm.1) | copy-start | bytes 196612

commit v3 on v2

--- a/solution.py
+++ b/solution.py
@@ -107,9 +107,9 @@
 
 def fused_kernel(
     wide, narrow,
-    x_hbm, t_hbm, rows_ref, cols_ref, count_ref, wn_hbm, wr_hbm, ow_hbm, cot_hbm,
+    x_hbm, t_hbm, rows_ref, cols_ref, count_hbm, wn_hbm, wr_hbm, ow_hbm, cot_hbm,
     grads_out, lo_out,
-    xf, tiles, ow, cot, wn, wr, dense, part, part_bf, pre_in, agg,
+    xf, tiles, ow, cot, wn, wr, count_ref, dense, part, hidden_grad, sent, came, pre_all, agg,
     pg, hid, grad32, grad, from_y, to_z, from_z, gall, lo,
     local_sem, send_sem, recv_sem,
 ):
@@ -171,6 +171,7 @@
         pltpu.make_async_copy(src, dst, local_sem.at[k])
         for k, (src, dst) in enumerate(
             (
+                (count_hbm, count_ref),
                 (t_hbm.at[0, 0], tiles),
                 (x_hbm, xf.at[me_b]),
                 (wr_hbm, wr),
@@ -182,8 +183,9 @@
     ]
     for copy in local:
         copy.start()
-    tile_copy, x_copy, wr_copy, wn_copy, cot_copy, ow_copy = local
-
+    count_copy, tile_copy, x_copy, wr_copy, wn_copy, cot_copy, ow_copy = local
+
+    count_copy.wait()
     live = count_ref[0, 0]
     chunk = 32
     positions = tile_rows_count * across
@@ -202,7 +204,9 @@
             )
 
         sums = lax.fori_loop(
-            0, slots, add_slot, tuple(jnp.zeros((chunk, side), f32) for _ in range(positions))
+            0, slots, add_slot,
+            tuple(jnp.zeros((chunk, side), f32) for _ in range(positions)),
+            unroll=4,
         )
         for p in range(positions):
             dense[me_n, p // across, at, pl.ds(p % across * side, side)] = sums[p].astype(bf16)
@@ -216,7 +220,12 @@
     pl.semaphore_wait(barrier, len(partners))
 
     z_order = sorted(range(1, z_size), key=lambda dz: abs(dz - z_size / 2))
-    blocks = {dz: send(x_hbm, xf.at[me_b], z_dev(dz)) for dz in z_order}
+    x_halves = [pl.ds(h * (node_rows // 2), node_rows // 2) for h in range(2)]
+    blocks = {
+        (dz, h): send(x_hbm.at[x_halves[h]], xf.at[me_b, x_halves[h]], z_dev(dz))
+        for h in range(2)
+        for dz in z_order
+    }
     y_blocks = [send(x_hbm, xf.at[me_b], y_dev)]
     dense_x = [send(half(me_n, 0), half(me_n, 0), (me_b, x_n))]
     dense_core = [send(half(me_n, 0), half(me_n, 0), (me_b, core_n))]
@@ -225,23 +234,24 @@
     dense_core.append(send(half(me_n, 1), half(me_n, 1), (me_b, core_n)))
     dense_fwd = []
 
-    def pass_block(dz):
-        blocks[dz].wait_recv()
-        b = z_source(dz)
-        y_blocks.append(send(xf.at[b], xf.at[b], y_dev))
+    def pass_block(dz, h):
+        blocks[dz, h].wait_recv()
+        part_of = xf.at[z_source(dz), x_halves[h]]
+        y_blocks.append(send(part_of, part_of, y_dev))
 
     def pass_half(h):
         dense_x[h].wait_recv()
         dense_fwd.append(send(half(x_n, h), half(x_n, h), (me_b, core_n)))
 
-    for dz in z_order[1:]:
-        pass_block(dz)
+    for dz in z_order[1:] + z_order[:1]:
+        pass_block(dz, 0)
     pass_half(0)
-    pass_block(z_order[0])
+    for dz in z_order[1:] + z_order[:1]:
+        pass_block(dz, 1)
     cot_copy.wait()
     ow_copy.wait()
-    hidden_grad = lax.dot_general(
-        cot[group_rows(me_n), :], ow[...], (((1,), (1,)), ((), ())), preferred_element_type=f32
+    hidden_grad[...] = lax.dot_general(
+        cot[...], ow[...], (((1,), (1,)), ((), ())), preferred_element_type=f32
     )
     pass_half(1)
     x_copy.wait()
@@ -268,32 +278,40 @@
     total = total + product(xc_n)
     agg[...] = total.astype(bf16)
 
-    arriving = []
-    narrow_partners = (xc_n, x_n, core_n)
-    for i, n in enumerate(narrow_partners):
-        at = group_rows(n)
-        there = part[at, :] + jnp.dot(agg[at, :], wn[...], preferred_element_type=f32)
-        part_bf[i] = there.astype(bf16)
-        arriving.append(send(part_bf.at[i], pre_in.at[i], (me_b, n)))
-    mine = group_rows(me_n)
-    pre = part[mine, :] + jnp.dot(agg[mine, :], wn[...], preferred_element_type=f32)
-    for i, copy in enumerate(arriving):
-        copy.wait_recv()
-        pre = pre + pre_in[i].astype(f32)
-    sig = jax.nn.sigmoid(pre)
-    pg[mine, :] = (hidden_grad * sig * (1.0 + pre * (1.0 - sig))).astype(bf16)
-    pg_x = send(pg.at[mine, :], pg.at[mine, :], (me_b, x_n))
-    pg_core = [send(pg.at[mine, :], pg.at[mine, :], (me_b, core_n))]
-    hid[mine, :] = (pre * sig).astype(bf16)
-    hid_x = send(hid.at[mine, :], hid.at[mine, :], (me_b, x_n))
-    hid_core = [send(hid.at[mine, :], hid.at[mine, :], (me_b, core_n))]
-    theirs = group_rows(x_n)
-    pg_x.wait_recv()
-    pg_core.append(send(pg.at[theirs, :], pg.at[theirs, :], (me_b, core_n)))
-    hid_x.wait_recv()
-    hid_core.append(send(hid.at[theirs, :], hid.at[theirs, :], (me_b, core_n)))
-    for copy in pg_core:
-        copy.wait_recv()
+    def pre_rows(core, q):
+        return pl.ds(pl.multiple_of(core * 2 * group + q * group, group), group)
+
+    def gates(rows, pre):
+        sig = jax.nn.sigmoid(pre)
+        pg[rows, :] = (hidden_grad[rows, :] * sig * (1.0 + pre * (1.0 - sig))).astype(bf16)
+        hid[rows, :] = (pre * sig).astype(bf16)
+
+    def half_pre(core):
+        rows = pl.ds(pl.multiple_of(core * 2 * group, group), 2 * group)
+        return part[rows, :] + jnp.dot(agg[rows, :], wn[...], preferred_element_type=f32)
+
+    my_core = me_n % CORES
+    sent[0] = half_pre(1 - my_core).astype(bf16).reshape(2, group, hidden_width)
+    to_core = [send(sent.at[0, q], came.at[0, q], (me_b, core_n)) for q in range(2)]
+    kept = half_pre(my_core).reshape(2, group, hidden_width)
+    kept = [kept[0], kept[1]]
+    to_x, back = [], []
+    for q in range(2):
+        to_core[q].wait_recv()
+        kept[q] = kept[q] + came[0, q].astype(f32)
+        sent[1, q] = kept[q].astype(bf16)
+        to_x.append(send(sent.at[1, q], came.at[1, q], (me_b, x_n)))
+    for q in range(2):
+        to_x[q].wait_recv()
+        pre = kept[q] + came[1, q].astype(f32)
+        rows = pre_rows(my_core, q)
+        pre_all[rows, :] = pre.astype(bf16)
+        back.append(send(pre_all.at[rows, :], pre_all.at[rows, :], (me_b, core_n)))
+        gates(rows, pre)
+    for q in range(2):
+        back[q].wait_recv()
+        rows = pre_rows(1 - my_core, q)
+        gates(rows, pre_all[rows, :].astype(f32))
 
     contract_rows = (((0,), (0,)), ((), ()))
     tracks = (pl.ds(0, 2), pl.ds(2, 1))
@@ -319,8 +337,6 @@
     fill(0, agg[...], pg[...])
     fill(1, xf[me_b], pg[...])
     halves = [to_other_y(0)]
-    for copy in hid_core:
-        copy.wait_recv()
     fill(2, cot[:, slice_cols(me_n)], hid[...])
     halves.append(to_other_y(1))
 
@@ -338,7 +354,7 @@
                 )
         sums.append(both)
     lo[...] = jnp.dot(hid[...], ow[:, slice_cols(me_n)], preferred_element_type=f32)
-    lo_copy = pltpu.make_async_copy(lo, lo_out, local_sem.at[6])
+    lo_copy = pltpu.make_async_copy(lo, lo_out, local_sem.at[7])
     lo_copy.start()
     last, done = [], []
     for track in range(2):
@@ -357,12 +373,20 @@
             last.append(send(gall.at[at], gall.at[at], y_dev))
     for copy in last:
         copy.wait_recv()
-    out_copy = pltpu.make_async_copy(gall, grads_out, local_sem.at[7])
+    out_copy = pltpu.make_async_copy(gall, grads_out, local_sem.at[8])
     out_copy.start()
     for copy in pending:
         copy.wait_send()
     lo_copy.wait()
     out_copy.wait()
+
+
+def finish_kernel(x_ref, product_ref, grads_ref, out_ref, neighbor_ref, root_ref, output_ref):
+    f32 = jnp.float32
+    out_ref[...] = (x_ref[...].astype(f32) + product_ref[...]).astype(out_ref.dtype)
+    neighbor_ref[...] = grads_ref[0].astype(f32)
+    root_ref[...] = grads_ref[1].astype(f32)
+    output_ref[...] = grads_ref[2].astype(f32).T
 
 
 def per_device_fused(
@@ -386,7 +410,7 @@
             jax.ShapeDtypeStruct((3, width, hidden_width), bf16),
             jax.ShapeDtypeStruct((node_rows, width), f32),
         ),
-        in_specs=[hbm, hbm, smem, smem, smem, hbm, hbm, hbm, hbm],
+        in_specs=[hbm, hbm, smem, smem, hbm, hbm, hbm, hbm, hbm],
         out_specs=(hbm, hbm),
         scratch_shapes=[
             pltpu.VMEM((wide, node_rows, width), bf16),
@@ -395,10 +419,13 @@
             pltpu.VMEM((node_rows, hidden_width), bf16),
             pltpu.VMEM((width, hidden_width), bf16),
             pltpu.VMEM((width, hidden_width), bf16),
+            pltpu.SMEM(tile_count.shape, jnp.int32),
             pltpu.VMEM((narrow, node_rows // side, side, wide * group), bf16),
             pltpu.VMEM((node_rows, hidden_width), f32),
-            pltpu.VMEM((narrow - 1, group, hidden_width), bf16),
-            pltpu.VMEM((narrow - 1, group, hidden_width), bf16),
+            pltpu.VMEM((node_rows, hidden_width), f32),
+            pltpu.VMEM((2, 2, group, hidden_width), bf16),
+            pltpu.VMEM((2, 2, group, hidden_width), bf16),
+            pltpu.VMEM((node_rows, hidden_width), bf16),
             pltpu.VMEM((node_rows, width), bf16),
             pltpu.VMEM((node_rows, hidden_width), bf16),
             pltpu.VMEM((node_rows, hidden_width), bf16),
@@ -409,7 +436,7 @@
             pltpu.VMEM((z_size, 3, piece, hidden_width), bf16),
             pltpu.VMEM((3, width, hidden_width), bf16),
             pltpu.VMEM((node_rows, width), f32),
-            pltpu.SemaphoreType.DMA((8,)),
+            pltpu.SemaphoreType.DMA((9,)),
             pltpu.SemaphoreType.DMA((copies,)),
             pltpu.SemaphoreType.DMA((copies,)),
         ],
@@ -420,13 +447,19 @@
         features, tile_blocks, tile_rows, tile_cols, tile_count,
         neighbor_weight, root_weight, output_weight, cotangent,
     )
-    layer_output = (features.astype(f32) + product).astype(bf16)
-    return (
-        layer_output,
-        grads[0].astype(f32),
-        grads[1].astype(f32),
-        grads[2].T.astype(f32),
-    )
+    vmem = pl.BlockSpec(memory_space=pltpu.VMEM)
+    return pl.pallas_call(
+        finish_kernel,
+        out_shape=(
+            jax.ShapeDtypeStruct((node_rows, width), bf16),
+            jax.ShapeDtypeStruct((width, hidden_width), f32),
+            jax.ShapeDtypeStruct((width, hidden_width), f32),
+            jax.ShapeDtypeStruct((hidden_width, width), f32),
+        ),
+        in_specs=[vmem] * 3,
+        out_specs=(vmem,) * 4,
+        compiler_params=pltpu.CompilerParams(vmem_limit_bytes=63 * 1024 * 1024),
+    )(features, product, grads)
 
 
 def solution(mesh):

time: 53.9 us -> 47.6 us (0.88)
  other arithmetic: 3.46 us -> 0 us
  Pallas kernels: 48 us -> 46.1 us
  local copies, waits for them, and re-layouts: 0.84 us -> 0 us
    pallas_call x1, Pallas kernels: 48 us -> 44.1 us  [per_device_fused(): pl.pallas_call(functools.partial(fused_kernel, wide, narrow), out_shape=(...]
    convert_element_type x2 -> x0, other arithmetic: 3.46 us -> none  [the longest x1 1.91 us: per_device_fused(): grads[2].T.astype(f32)]
    pallas_call x0 -> x1, Pallas kernels: none -> 2.04 us  [per_device_fused(): pl.pallas_call(finish_kernel, out_shape=(jax.ShapeDtypeStruct((node_rows,...]
    unnamed x3 -> x0, local copies, waits for them, and re-layouts: 0.84 us -> none
where the time goes in v3:
time: 47.6 us; the launch traced here: 47.4 us
  Pallas kernels  46.1 us (97%)
  between operations  1.29 us (3%)
    pallas_call x1, Pallas kernels, per_device_fused(): pl.pallas_call(functools.partial(fused_kernel, wide, narrow), out_shape=(...  44.1 us
    pallas_call x1, Pallas kernels, per_device_fused(): pl.pallas_call(finish_kernel, out_shape=(jax.ShapeDtypeStruct((node_rows,...  2.04 us

profile of v3, /device:TPU:0, one launch (start us, length us, event | category | flops | bytes accessed | tf_op | source)
XLA Modules:
  0.0 47.4 jit_solution(1504729852204067103)
XLA Ops:
  1.3 44.1 %shard_map.120 = (bf16[3,128,512]{2,1,0:T(8,128)(2,1)}, f32[256,128]{1,0:T(8,128)}) custom-call(bf16[256,128]{1,0:T(8,128)(2,1)} %x_ref.1, bf16[1,1,48,128,128]{4,3,2,1,0:T(8,128)(2,1)} %t_hbm.1, s32[1,1,48]{2,1,0:T(1,128)} %rows_ref.1, s32[1,1,48]{2,1,0:T(1,128)} %cols_ref.1, s32[1,1]{1,0:T(1,128)S(6)} %copy.13.count_hbm, bf16[128,512]{1,0:T(8,128)(2,1)} %wn_hbm.1, ...), custom_call_target="tpu_custom_call" | custom-call | tf_op jit(solution)/shard_map/pallas_call | solution.py:407
  45.3 2.0 %shard_map.121 = (bf16[256,128]{1,0:T(8,128)(2,1)}, f32[128,512]{1,0:T(8,128)}, f32[128,512]{1,0:T(8,128)}, f32[512,128]{1,0:T(8,128)}) custom-call(bf16[256,128]{1,0:T(8,128)(2,1)} %x_ref.1, f32[256,128]{1,0:T(8,128)} %get-tuple-element.6.product_ref, bf16[3,128,512]{2,1,0:T(8,128)(2,1)} %get-tuple-element.7.grads_ref), custom_call_target="tpu_custom_call" | custom-call | tf_op jit(solution)/shard_map/pallas_call | solution.py:451

commit v4 on v3

--- a/solution.py
+++ b/solution.py
@@ -191,8 +191,8 @@
     positions = tile_rows_count * across
     steps = side // chunk
 
-    def densify(step, _):
-        at = pl.ds(pl.multiple_of(step * chunk, chunk), chunk)
+    def densify(step):
+        at = pl.ds(step * chunk, chunk)
 
         def add_slot(s, sums):
             tile = tiles[s, at, :].astype(f32)
@@ -210,15 +210,11 @@
         )
         for p in range(positions):
             dense[me_n, p // across, at, pl.ds(p % across * side, side)] = sums[p].astype(bf16)
-        return 0
-
-    def half(n, h):
-        return dense.at[n, :, pl.ds(h * (side // 2), side // 2), :]
-
-    tile_copy.wait()
-    lax.fori_loop(0, steps // 2, densify, 0)
+
+    def slab(n, step):
+        return dense.at[n, :, pl.ds(step * chunk, chunk), :]
+
     pl.semaphore_wait(barrier, len(partners))
-
     z_order = sorted(range(1, z_size), key=lambda dz: abs(dz - z_size / 2))
     x_halves = [pl.ds(h * (node_rows // 2), node_rows // 2) for h in range(2)]
     blocks = {
@@ -227,33 +223,35 @@
         for dz in z_order
     }
     y_blocks = [send(x_hbm, xf.at[me_b], y_dev)]
-    dense_x = [send(half(me_n, 0), half(me_n, 0), (me_b, x_n))]
-    dense_core = [send(half(me_n, 0), half(me_n, 0), (me_b, core_n))]
-    lax.fori_loop(steps // 2, steps, densify, 0)
-    dense_x.append(send(half(me_n, 1), half(me_n, 1), (me_b, x_n)))
-    dense_core.append(send(half(me_n, 1), half(me_n, 1), (me_b, core_n)))
-    dense_fwd = []
+    tile_copy.wait()
+    dense_x, dense_core, dense_fwd = [], [], []
+    for step in range(steps):
+        densify(step)
+        dense_x.append(send(slab(me_n, step), slab(me_n, step), (me_b, x_n)))
+        dense_core.append(send(slab(me_n, step), slab(me_n, step), (me_b, core_n)))
 
     def pass_block(dz, h):
         blocks[dz, h].wait_recv()
         part_of = xf.at[z_source(dz), x_halves[h]]
         y_blocks.append(send(part_of, part_of, y_dev))
 
-    def pass_half(h):
-        dense_x[h].wait_recv()
-        dense_fwd.append(send(half(x_n, h), half(x_n, h), (me_b, core_n)))
+    def pass_slab(step):
+        dense_x[step].wait_recv()
+        dense_fwd.append(send(slab(x_n, step), slab(x_n, step), (me_b, core_n)))
 
     for dz in z_order[1:] + z_order[:1]:
         pass_block(dz, 0)
-    pass_half(0)
-    for dz in z_order[1:] + z_order[:1]:
-        pass_block(dz, 1)
+    for step in range(steps // 2):
+        pass_slab(step)
     cot_copy.wait()
     ow_copy.wait()
     hidden_grad[...] = lax.dot_general(
         cot[...], ow[...], (((1,), (1,)), ((), ())), preferred_element_type=f32
     )
-    pass_half(1)
+    for dz in z_order[1:] + z_order[:1]:
+        pass_block(dz, 1)
+    for step in range(steps // 2, steps):
+        pass_slab(step)
     x_copy.wait()
     wr_copy.wait()
     wn_copy.wait()

time: 47.6 us -> 46.3 us (0.973)
  Pallas kernels: 46.1 us -> 44.8 us
    pallas_call x1, Pallas kernels: 44.1 us -> 42.8 us  [per_device_fused(): pl.pallas_call(functools.partial(fused_kernel, wide, narrow), out_shape=(...]
where the time goes in v4:
time: 46.3 us; the launch traced here: 46.1 us
  Pallas kernels  44.8 us (97%)
  between operations  1.29 us (3%)
    pallas_call x1, Pallas kernels, per_device_fused(): pl.pallas_call(functools.partial(fused_kernel, wide, narrow), out_shape=(...  42.8 us
    pallas_call x1, Pallas kernels, per_device_fused(): pl.pallas_call(finish_kernel, out_shape=(jax.ShapeDtypeStruct((node_rows,...  2.04 us

profile of v4, /device:TPU:0, one launch (start us, length us, event | category | flops | bytes accessed | tf_op | source)
XLA Modules:
  0.0 46.1 jit_solution(9648476109226060699)
XLA Ops:
  1.3 42.8 %shard_map.120 = (bf16[3,128,512]{2,1,0:T(8,128)(2,1)}, f32[256,128]{1,0:T(8,128)}) custom-call(bf16[256,128]{1,0:T(8,128)(2,1)} %x_ref.1, bf16[1,1,48,128,128]{4,3,2,1,0:T(8,128)(2,1)} %t_hbm.1, s32[1,1,48]{2,1,0:T(1,128)} %rows_ref.1, s32[1,1,48]{2,1,0:T(1,128)} %cols_ref.1, s32[1,1]{1,0:T(1,128)S(6)} %copy.13.count_hbm, bf16[128,512]{1,0:T(8,128)(2,1)} %wn_hbm.1, ...), custom_call_target="tpu_custom_call" | custom-call | tf_op jit(solution)/shard_map/pallas_call | solution.py:405
  44.0 2.0 %shard_map.121 = (bf16[256,128]{1,0:T(8,128)(2,1)}, f32[128,512]{1,0:T(8,128)}, f32[128,512]{1,0:T(8,128)}, f32[512,128]{1,0:T(8,128)}) custom-call(bf16[256,128]{1,0:T(8,128)(2,1)} %x_ref.1, f32[256,128]{1,0:T(8,128)} %get-tuple-element.6.product_ref, bf16[3,128,512]{2,1,0:T(8,128)(2,1)} %get-tuple-element.7.grads_ref), custom_call_target="tpu_custom_call" | custom-call | tf_op jit(solution)/shard_map/pallas_call | solution.py:449

commit v5 on v4

--- a/solution.py
+++ b/solution.py
@@ -312,7 +312,7 @@
         gates(rows, pre_all[rows, :].astype(f32))
 
     contract_rows = (((0,), (0,)), ((), ()))
-    tracks = (pl.ds(0, 2), pl.ds(2, 1))
+    tracks = [pl.ds(k, 1) for k in range(3)]
 
     def piece_of(track, b):
         return (tracks[track], pl.ds(pl.multiple_of(b * piece, piece), piece), slice(None))
@@ -332,14 +332,14 @@
             for dz in z_order + [0]
         ]
 
-    fill(0, agg[...], pg[...])
-    fill(1, xf[me_b], pg[...])
-    halves = [to_other_y(0)]
-    fill(2, cot[:, slice_cols(me_n)], hid[...])
-    halves.append(to_other_y(1))
+    halves = []
+    operands = ((agg[...], pg[...]), (xf[me_b], pg[...]), (cot[:, slice_cols(me_n)], hid[...]))
+    for track, (left, right) in enumerate(operands):
+        fill(track, left, right)
+        halves.append(to_other_y(track))
 
     sums, arriving_z = [], []
-    for track in range(2):
+    for track in range(3):
         along = tracks[track]
         arriving_z.append([])
         for dz, copy in zip(z_order + [0], halves[track]):
@@ -355,7 +355,7 @@
     lo_copy = pltpu.make_async_copy(lo, lo_out, local_sem.at[7])
     lo_copy.start()
     last, done = [], []
-    for track in range(2):
+    for track in range(3):
         both = sums[track]
         for dz, copy in arriving_z[track]:
             copy.wait_recv()
@@ -364,7 +364,7 @@
         gall[own] = both.astype(bf16)
         done.append({dz: send(gall.at[own], gall.at[own], z_dev(dz)) for dz in z_order})
         last.append(send(gall.at[own], gall.at[own], y_dev))
-    for track in range(2):
+    for track in range(3):
         for dz in z_order[1:] + z_order[:1]:
             done[track][dz].wait_recv()
             at = piece_of(track, z_source(dz))
@@ -379,12 +379,39 @@
     out_copy.wait()
 
 
-def finish_kernel(x_ref, product_ref, grads_ref, out_ref, neighbor_ref, root_ref, output_ref):
+def finish_kernel(
+    x_hbm, product_hbm, grads_hbm, out_hbm, neighbor_hbm, root_hbm, output_hbm,
+    x, product, grads, out, neighbor, root, output, in_sem, out_sem,
+):
     f32 = jnp.float32
-    out_ref[...] = (x_ref[...].astype(f32) + product_ref[...]).astype(out_ref.dtype)
-    neighbor_ref[...] = grads_ref[0].astype(f32)
-    root_ref[...] = grads_ref[1].astype(f32)
-    output_ref[...] = grads_ref[2].astype(f32).T
+    pairs = [(grads_hbm.at[k], grads.at[k]) for k in (2, 0, 1)]
+    pairs += [(x_hbm, x), (product_hbm, product)]
+    arriving = [
+        pltpu.make_async_copy(src, dst, in_sem.at[k]) for k, (src, dst) in enumerate(pairs)
+    ]
+    for copy in arriving:
+        copy.start()
+    leaving = [
+        pltpu.make_async_copy(src, dst, out_sem.at[k])
+        for k, (src, dst) in enumerate(
+            ((output, output_hbm), (neighbor, neighbor_hbm), (root, root_hbm), (out, out_hbm))
+        )
+    ]
+    arriving[0].wait()
+    output[...] = grads[2].astype(f32).T
+    leaving[0].start()
+    arriving[1].wait()
+    neighbor[...] = grads[0].astype(f32)
+    leaving[1].start()
+    arriving[2].wait()
+    root[...] = grads[1].astype(f32)
+    leaving[2].start()
+    arriving[3].wait()
+    arriving[4].wait()
+    out[...] = (x[...].astype(f32) + product[...]).astype(out.dtype)
+    leaving[3].start()
+    for copy in leaving:
+        copy.wait()
 
 
 def per_device_fused(
@@ -399,7 +426,7 @@
     z_size = wide // Y_SIZE
     piece = width // wide
     bf16, f32 = jnp.bfloat16, jnp.float32
-    copies = 64
+    copies = 96
     hbm = pl.BlockSpec(memory_space=pltpu.HBM)
     smem = pl.BlockSpec(memory_space=pltpu.SMEM)
     grads, product = pl.pallas_call(
@@ -445,7 +472,6 @@
         features, tile_blocks, tile_rows, tile_cols, tile_count,
         neighbor_weight, root_weight, output_weight, cotangent,
     )
-    vmem = pl.BlockSpec(memory_space=pltpu.VMEM)
     return pl.pallas_call(
         finish_kernel,
         out_shape=(
@@ -454,8 +480,19 @@
             jax.ShapeDtypeStruct((width, hidden_width), f32),
             jax.ShapeDtypeStruct((hidden_width, width), f32),
         ),
-        in_specs=[vmem] * 3,
-        out_specs=(vmem,) * 4,
+        in_specs=[hbm] * 3,
+        out_specs=(hbm,) * 4,
+        scratch_shapes=[
+            pltpu.VMEM((node_rows, width), bf16),
+            pltpu.VMEM((node_rows, width), f32),
+            pltpu.VMEM((3, width, hidden_width), bf16),
+            pltpu.VMEM((node_rows, width), bf16),
+            pltpu.VMEM((width, hidden_width), f32),
+            pltpu.VMEM((width, hidden_width), f32),
+            pltpu.VMEM((hidden_width, width), f32),
+            pltpu.SemaphoreType.DMA((5,)),
+            pltpu.SemaphoreType.DMA((4,)),
+        ],
         compiler_params=pltpu.CompilerParams(vmem_limit_bytes=63 * 1024 * 1024),
     )(features, product, grads)
 

time: 46.3 us -> 46.9 us (1.013)
  Pallas kernels: 44.8 us -> 45.4 us
    pallas_call x1, Pallas kernels: 42.8 us -> 43.4 us  [per_device_fused(): pl.pallas_call(functools.partial(fused_kernel, wide, narrow), out_shape=(...]
where the time goes in v5:
time: 46.9 us; the launch traced here: 46.7 us
  Pallas kernels  45.4 us (97%)
  between operations  1.29 us (3%)
    pallas_call x1, Pallas kernels, per_device_fused(): pl.pallas_call(functools.partial(fused_kernel, wide, narrow), out_shape=(...  43.4 us
    pallas_call x1, Pallas kernels, per_device_fused(): pl.pallas_call(finish_kernel, out_shape=(jax.ShapeDtypeStruct((node_rows,...  1.98 us

profile of v5, /device:TPU:0, one launch (start us, length us, event | category | flops | bytes accessed | tf_op | source)
XLA Modules:
  0.0 46.7 jit_solution(17443558275504628437)
XLA Ops:
  1.3 43.4 %shard_map.120 = (bf16[3,128,512]{2,1,0:T(8,128)(2,1)}, f32[256,128]{1,0:T(8,128)}) custom-call(bf16[256,128]{1,0:T(8,128)(2,1)} %x_hbm.3, bf16[1,1,48,128,128]{4,3,2,1,0:T(8,128)(2,1)} %t_hbm.1, s32[1,1,48]{2,1,0:T(1,128)} %rows_ref.1, s32[1,1,48]{2,1,0:T(1,128)} %cols_ref.1, s32[1,1]{1,0:T(1,128)S(6)} %copy.13.count_hbm, bf16[128,512]{1,0:T(8,128)(2,1)} %wn_hbm.1, ...), custom_call_target="tpu_custom_call" | custom-call | tf_op jit(solution)/shard_map/pallas_call | solution.py:432
  44.7 2.0 %shard_map.121 = (bf16[256,128]{1,0:T(8,128)(2,1)}, f32[128,512]{1,0:T(8,128)}, f32[128,512]{1,0:T(8,128)}, f32[512,128]{1,0:T(8,128)}) custom-call(bf16[256,128]{1,0:T(8,128)(2,1)} %x_hbm.3, f32[256,128]{1,0:T(8,128)} %get-tuple-element.6.product_hbm, bf16[3,128,512]{2,1,0:T(8,128)(2,1)} %get-tuple-element.7.grads_hbm), custom_call_target="tpu_custom_call" | custom-call | tf_op jit(solution)/shard_map/pallas_call | solution.py:475

commit v6 on v5

--- a/solution.py
+++ b/solution.py
@@ -312,7 +312,7 @@
         gates(rows, pre_all[rows, :].astype(f32))
 
     contract_rows = (((0,), (0,)), ((), ()))
-    tracks = [pl.ds(k, 1) for k in range(3)]
+    tracks = [pl.ds(0, 3)]
 
     def piece_of(track, b):
         return (tracks[track], pl.ds(pl.multiple_of(b * piece, piece), piece), slice(None))
@@ -334,12 +334,12 @@
 
     halves = []
     operands = ((agg[...], pg[...]), (xf[me_b], pg[...]), (cot[:, slice_cols(me_n)], hid[...]))
-    for track, (left, right) in enumerate(operands):
-        fill(track, left, right)
-        halves.append(to_other_y(track))
+    for k, (left, right) in enumerate(operands):
+        fill(k, left, right)
+    halves.append(to_other_y(0))
 
     sums, arriving_z = [], []
-    for track in range(3):
+    for track in range(1):
         along = tracks[track]
         arriving_z.append([])
         for dz, copy in zip(z_order + [0], halves[track]):
@@ -355,7 +355,7 @@
     lo_copy = pltpu.make_async_copy(lo, lo_out, local_sem.at[7])
     lo_copy.start()
     last, done = [], []
-    for track in range(3):
+    for track in range(1):
         both = sums[track]
         for dz, copy in arriving_z[track]:
             copy.wait_recv()
@@ -364,7 +364,7 @@
         gall[own] = both.astype(bf16)
         done.append({dz: send(gall.at[own], gall.at[own], z_dev(dz)) for dz in z_order})
         last.append(send(gall.at[own], gall.at[own], y_dev))
-    for track in range(3):
+    for track in range(1):
         for dz in z_order[1:] + z_order[:1]:
             done[track][dz].wait_recv()
             at = piece_of(track, z_source(dz))

time: 46.9 us -> 48.2 us (1.028)
  Pallas kernels: 45.4 us -> 46.7 us
    pallas_call x1, Pallas kernels: 43.4 us -> 44.7 us  [per_device_fused(): pl.pallas_call(functools.partial(fused_kernel, wide, narrow), out_shape=(...]
where the time goes in v6:
time: 48.2 us; the launch traced here: 48 us
  Pallas kernels  46.7 us (97%)
  between operations  1.29 us (3%)
    pallas_call x1, Pallas kernels, per_device_fused(): pl.pallas_call(functools.partial(fused_kernel, wide, narrow), out_shape=(...  44.7 us
    pallas_call x1, Pallas kernels, per_device_fused(): pl.pallas_call(finish_kernel, out_shape=(jax.ShapeDtypeStruct((node_rows,...  1.98 us

profile of v6, /device:TPU:0, one launch (start us, length us, event | category | flops | bytes accessed | tf_op | source)
XLA Modules:
  0.0 48.0 jit_solution(9122680179859814799)
XLA Ops:
  1.3 44.7 %shard_map.120 = (bf16[3,128,512]{2,1,0:T(8,128)(2,1)}, f32[256,128]{1,0:T(8,128)}) custom-call(bf16[256,128]{1,0:T(8,128)(2,1)} %x_hbm.3, bf16[1,1,48,128,128]{4,3,2,1,0:T(8,128)(2,1)} %t_hbm.1, s32[1,1,48]{2,1,0:T(1,128)} %rows_ref.1, s32[1,1,48]{2,1,0:T(1,128)} %cols_ref.1, s32[1,1]{1,0:T(1,128)S(6)} %copy.13.count_hbm, bf16[128,512]{1,0:T(8,128)(2,1)} %wn_hbm.1, ...), custom_call_target="tpu_custom_call" | custom-call | tf_op jit(solution)/shard_map/pallas_call | solution.py:432
  46.0 2.0 %shard_map.121 = (bf16[256,128]{1,0:T(8,128)(2,1)}, f32[128,512]{1,0:T(8,128)}, f32[128,512]{1,0:T(8,128)}, f32[512,128]{1,0:T(8,128)}) custom-call(bf16[256,128]{1,0:T(8,128)(2,1)} %x_hbm.3, f32[256,128]{1,0:T(8,128)} %get-tuple-element.6.product_hbm, bf16[3,128,512]{2,1,0:T(8,128)(2,1)} %get-tuple-element.7.grads_hbm), custom_call_target="tpu_custom_call" | custom-call | tf_op jit(solution)/shard_map/pallas_call | solution.py:475

commit v7 on v6

--- a/solution.py
+++ b/solution.py
@@ -243,11 +243,6 @@
         pass_block(dz, 0)
     for step in range(steps // 2):
         pass_slab(step)
-    cot_copy.wait()
-    ow_copy.wait()
-    hidden_grad[...] = lax.dot_general(
-        cot[...], ow[...], (((1,), (1,)), ((), ())), preferred_element_type=f32
-    )
     for dz in z_order[1:] + z_order[:1]:
         pass_block(dz, 1)
     for step in range(steps // 2, steps):
@@ -299,6 +294,11 @@
         kept[q] = kept[q] + came[0, q].astype(f32)
         sent[1, q] = kept[q].astype(bf16)
         to_x.append(send(sent.at[1, q], came.at[1, q], (me_b, x_n)))
+    cot_copy.wait()
+    ow_copy.wait()
+    hidden_grad[...] = lax.dot_general(
+        cot[...], ow[...], (((1,), (1,)), ((), ())), preferred_element_type=f32
+    )
     for q in range(2):
         to_x[q].wait_recv()
         pre = kept[q] + came[1, q].astype(f32)
@@ -312,7 +312,7 @@
         gates(rows, pre_all[rows, :].astype(f32))
 
     contract_rows = (((0,), (0,)), ((), ()))
-    tracks = [pl.ds(0, 3)]
+    tracks = (pl.ds(0, 2), pl.ds(2, 1))
 
     def piece_of(track, b):
         return (tracks[track], pl.ds(pl.multiple_of(b * piece, piece), piece), slice(None))
@@ -336,10 +336,11 @@
     operands = ((agg[...], pg[...]), (xf[me_b], pg[...]), (cot[:, slice_cols(me_n)], hid[...]))
     for k, (left, right) in enumerate(operands):
         fill(k, left, right)
-    halves.append(to_other_y(0))
+        if k:
+            halves.append(to_other_y(k - 1))
 
     sums, arriving_z = [], []
-    for track in range(1):
+    for track in range(2):
         along = tracks[track]
         arriving_z.append([])
         for dz, copy in zip(z_order + [0], halves[track]):
@@ -355,7 +356,7 @@
     lo_copy = pltpu.make_async_copy(lo, lo_out, local_sem.at[7])
     lo_copy.start()
     last, done = [], []
-    for track in range(1):
+    for track in range(2):
         both = sums[track]
         for dz, copy in arriving_z[track]:
             copy.wait_recv()
@@ -364,7 +365,7 @@
         gall[own] = both.astype(bf16)
         done.append({dz: send(gall.at[own], gall.at[own], z_dev(dz)) for dz in z_order})
         last.append(send(gall.at[own], gall.at[own], y_dev))
-    for track in range(1):
+    for track in range(2):
         for dz in z_order[1:] + z_order[:1]:
             done[track][dz].wait_recv()
             at = piece_of(track, z_source(dz))

time: 48.2 us -> 46.6 us (0.967)
  Pallas kernels: 46.7 us -> 45.1 us
    pallas_call x1, Pallas kernels: 44.7 us -> 43.2 us  [per_device_fused(): pl.pallas_call(functools.partial(fused_kernel, wide, narrow), out_shape=(...]
where the time goes in v7:
time: 46.6 us; the launch traced here: 46.4 us
  Pallas kernels  45.1 us (97%)
  between operations  1.29 us (3%)
    pallas_call x1, Pallas kernels, per_device_fused(): pl.pallas_call(functools.partial(fused_kernel, wide, narrow), out_shape=(...  43.2 us
    pallas_call x1, Pallas kernels, per_device_fused(): pl.pallas_call(finish_kernel, out_shape=(jax.ShapeDtypeStruct((node_rows,...  1.98 us

profile of v7, /device:TPU:0, one launch (start us, length us, event | category | flops | bytes accessed | tf_op | source)
XLA Modules:
  0.0 46.4 jit_solution(15222539769329149758)
XLA Ops:
  1.3 43.2 %shard_map.120 = (bf16[3,128,512]{2,1,0:T(8,128)(2,1)}, f32[256,128]{1,0:T(8,128)}) custom-call(bf16[256,128]{1,0:T(8,128)(2,1)} %x_hbm.3, bf16[1,1,48,128,128]{4,3,2,1,0:T(8,128)(2,1)} %t_hbm.1, s32[1,1,48]{2,1,0:T(1,128)} %rows_ref.1, s32[1,1,48]{2,1,0:T(1,128)} %cols_ref.1, s32[1,1]{1,0:T(1,128)S(6)} %copy.13.count_hbm, bf16[128,512]{1,0:T(8,128)(2,1)} %wn_hbm.1, ...), custom_call_target="tpu_custom_call" | custom-call | tf_op jit(solution)/shard_map/pallas_call | solution.py:433
  44.5 2.0 %shard_map.121 = (bf16[256,128]{1,0:T(8,128)(2,1)}, f32[128,512]{1,0:T(8,128)}, f32[128,512]{1,0:T(8,128)}, f32[512,128]{1,0:T(8,128)}) custom-call(bf16[256,128]{1,0:T(8,128)(2,1)} %x_hbm.3, f32[256,128]{1,0:T(8,128)} %get-tuple-element.6.product_hbm, bf16[3,128,512]{2,1,0:T(8,128)(2,1)} %get-tuple-element.7.grads_hbm), custom_call_target="tpu_custom_call" | custom-call | tf_op jit(solution)/shard_map/pallas_call | solution.py:476

commit v8 on v7

--- a/solution.py
+++ b/solution.py
@@ -216,10 +216,10 @@
 
     pl.semaphore_wait(barrier, len(partners))
     z_order = sorted(range(1, z_size), key=lambda dz: abs(dz - z_size / 2))
-    x_halves = [pl.ds(h * (node_rows // 2), node_rows // 2) for h in range(2)]
+    x_halves = [pl.ds(0, node_rows)]
     blocks = {
         (dz, h): send(x_hbm.at[x_halves[h]], xf.at[me_b, x_halves[h]], z_dev(dz))
-        for h in range(2)
+        for h in range(1)
         for dz in z_order
     }
     y_blocks = [send(x_hbm, xf.at[me_b], y_dev)]
@@ -239,12 +239,10 @@
         dense_x[step].wait_recv()
         dense_fwd.append(send(slab(x_n, step), slab(x_n, step), (me_b, core_n)))
 
-    for dz in z_order[1:] + z_order[:1]:
-        pass_block(dz, 0)
     for step in range(steps // 2):
         pass_slab(step)
     for dz in z_order[1:] + z_order[:1]:
-        pass_block(dz, 1)
+        pass_block(dz, 0)
     for step in range(steps // 2, steps):
         pass_slab(step)
     x_copy.wait()

time: 46.6 us -> 47.6 us (1.021)
  Pallas kernels: 45.1 us -> 46.1 us
    pallas_call x1, Pallas kernels: 43.2 us -> 44.1 us  [per_device_fused(): pl.pallas_call(functools.partial(fused_kernel, wide, narrow), out_shape=(...]
where the time goes in v8:
time: 47.6 us; the launch traced here: 47.4 us
  Pallas kernels  46.1 us (97%)
  between operations  1.29 us (3%)
    pallas_call x1, Pallas kernels, per_device_fused(): pl.pallas_call(functools.partial(fused_kernel, wide, narrow), out_shape=(...  44.1 us
    pallas_call x1, Pallas kernels, per_device_fused(): pl.pallas_call(finish_kernel, out_shape=(jax.ShapeDtypeStruct((node_rows,...  1.98 us

profile of v8, /device:TPU:0, one launch (start us, length us, event | category | flops | bytes accessed | tf_op | source)
XLA Modules:
  0.0 47.4 jit_solution(8247465476075289832)
XLA Ops:
  1.3 44.1 %shard_map.120 = (bf16[3,128,512]{2,1,0:T(8,128)(2,1)}, f32[256,128]{1,0:T(8,128)}) custom-call(bf16[256,128]{1,0:T(8,128)(2,1)} %x_hbm.3, bf16[1,1,48,128,128]{4,3,2,1,0:T(8,128)(2,1)} %t_hbm.1, s32[1,1,48]{2,1,0:T(1,128)} %rows_ref.1, s32[1,1,48]{2,1,0:T(1,128)} %cols_ref.1, s32[1,1]{1,0:T(1,128)S(6)} %copy.13.count_hbm, bf16[128,512]{1,0:T(8,128)(2,1)} %wn_hbm.1, ...), custom_call_target="tpu_custom_call" | custom-call | tf_op jit(solution)/shard_map/pallas_call | solution.py:431
  45.4 2.0 %shard_map.121 = (bf16[256,128]{1,0:T(8,128)(2,1)}, f32[128,512]{1,0:T(8,128)}, f32[128,512]{1,0:T(8,128)}, f32[512,128]{1,0:T(8,128)}) custom-call(bf16[256,128]{1,0:T(8,128)(2,1)} %x_hbm.3, f32[256,128]{1,0:T(8,128)} %get-tuple-element.6.product_hbm, bf16[3,128,512]{2,1,0:T(8,128)(2,1)} %get-tuple-element.7.grads_hbm), custom_call_target="tpu_custom_call" | custom-call | tf_op jit(solution)/shard_map/pallas_call | solution.py:474
